TPU v7x, 256 devices: a whole 4x4x8 slice. The times are simulated.
256 devices in a mesh: seq: 64 (over z, y, core), head: 4 (over x).
Axes of the slice: x: 4, y: 4, z: 8, core: 2. Of those that a mesh axis runs over, the one named last changes fastest.
Arguments:
- query_latent: bfloat16 [16384, 128, 576], P('seq', 'head'), may hold values from -16 to 16
- stretch_latent: bfloat16 [16384, 576], P('seq'), may hold values from -8 to 8
- cache_latent: bfloat16 [32768, 576], P('seq'), may hold values from -8 to 8
- query_index: bfloat16 [16384, 64, 128], P('seq', 'head'), may hold values from -8 to 8
- stretch_index: bfloat16 [16384, 128], P('seq'), may hold values from -8 to 8
- cache_index: bfloat16 [32768, 128], P('seq'), may hold values from -8 to 8
- index_gains: float32 [16384, 64], P('seq', 'head'), may hold values from -0.15 to 0.15
- block_ids: int32 [256, 7], P('seq'), may hold values from 0 to 511, as said below
Outputs:
- divergence: float32 [16384], P('seq')
- query_index_grad: bfloat16 [16384, 64, 128], P('seq', 'head')
- index_gains_grad: float32 [16384, 64], P('seq', 'head')
- cache_index_grad: float32 [32768, 128], P('seq')
- stretch_index_grad: float32 [16384, 128], P('seq')
Inputs may be any that keep to these rules, and one draw needn't show every extreme that they name: `block_ids`: the 7 entries of a row are distinct cached blocks. Over the 4 consecutive rows starting at a multiple of 4, at most 1 entries name blocks of one group o*8 to o*8 + 7, those entries are distinct, and some group is named exactly 1 times.
All inputs are finite; a program needn't handle non-finite values.
Results may differ from a plain program's by a relative error of at most 0.0065.
Values may be sent and summed in bfloat16 or wider, within the bound.
A program may use at most 128 MiB of HBM per device.

v0:
```python
import jax
import jax.numpy as jnp
from jax import lax
from jax.sharding import PartitionSpec as P

HEADS = 128


score_scale = 192.0 ** (-0.5)


def attention_mass(scores, allowed):
    masked = jnp.where(jnp.expand_dims(allowed, -2), scores, -jnp.inf)
    row_max = jnp.max(masked, axis=-1, keepdims=True)
    shifted = jnp.exp(masked - row_max)
    attention = shifted / jnp.sum(shifted, axis=-1, keepdims=True)
    return jnp.sum(attention, axis=-2)


def kl_terms(mass_sum, logits, allowed):
    target = mass_sum / HEADS
    masked = jnp.where(allowed, logits, -jnp.inf)
    row_max = jnp.max(masked, axis=-1, keepdims=True)
    shifted = jnp.exp(masked - row_max)
    total = jnp.sum(shifted, axis=-1, keepdims=True)
    model = shifted / total
    log_model = jnp.where(allowed, masked - row_max - jnp.log(total), 0.0)
    safe_target = jnp.where(target > 0, target, 1.0)
    pointwise = jnp.where(allowed, target * (jnp.log(safe_target) - log_model), 0.0)
    divergence = jnp.sum(pointwise, axis=-1)
    logit_gradient = jnp.where(allowed, model - target, 0.0)
    return (divergence, logit_gradient)


def per_device(
    query_latent,
    stretch_latent,
    cache_latent,
    query_index,
    stretch_index,
    cache_index,
    index_gains,
    block_ids,
):
    seq_count = lax.axis_size("seq")
    qblocks, picked_count = block_ids.shape
    row_count = query_latent.shape[0]
    block_len = row_count // qblocks
    key_width = cache_latent.shape[1]
    index_width = cache_index.shape[1]
    cache_blocks = cache_latent.shape[0] // block_len
    slot_count = qblocks * picked_count
    capacity = (slot_count + seq_count - 1) // seq_count
    span = (picked_count + 1) * block_len
    flat_ids = block_ids.reshape(slot_count)
    owners = flat_ids // cache_blocks
    local_ids = flat_ids % cache_blocks
    same_owner = owners[:, None] == owners[None, :]
    earlier = jnp.arange(slot_count)[None, :] < jnp.arange(slot_count)[:, None]
    slot_rank = jnp.sum(same_owner & earlier, axis=1)
    places = owners * capacity + slot_rank
    hits = places[:, None] == jnp.arange(seq_count * capacity)[None, :]
    request = jnp.sum(jnp.where(hits, local_ids[:, None] + 1, 0), axis=0) - 1
    incoming = lax.all_to_all(
        request.reshape(seq_count, capacity), "seq", split_axis=0, concat_axis=0, tiled=True
    )
    wanted = incoming.reshape(seq_count * capacity)
    filled = wanted >= 0
    clipped = jnp.maximum(wanted, 0)
    latent_blocks = cache_latent.reshape(cache_blocks, block_len, key_width)
    index_blocks = cache_index.reshape(cache_blocks, block_len, index_width)
    served_latent = jnp.where(filled[:, None, None], jnp.take(latent_blocks, clipped, axis=0), 0)
    served_latent = served_latent.reshape(seq_count, capacity, block_len, key_width)
    served_index = jnp.where(filled[:, None, None], jnp.take(index_blocks, clipped, axis=0), 0)
    served_index = served_index.reshape(seq_count, capacity, block_len, index_width)
    got_latent, got_index = (
        lax.all_to_all(served_latent, "seq", split_axis=0, concat_axis=0, tiled=True),
        lax.all_to_all(served_index, "seq", split_axis=0, concat_axis=0, tiled=True),
    )
    picked_latent = jnp.take(
        got_latent.reshape(seq_count * capacity, block_len, key_width), places, axis=0
    )
    latent_key_rows = jnp.concatenate(
        [
            picked_latent.reshape(qblocks, picked_count * block_len, key_width),
            stretch_latent.reshape(qblocks, block_len, key_width),
        ],
        axis=1,
    )
    picked_index = jnp.take(
        got_index.reshape(seq_count * capacity, block_len, index_width), places, axis=0
    )
    indexer_key_rows = jnp.concatenate(
        [
            picked_index.reshape(qblocks, picked_count * block_len, index_width),
            stretch_index.reshape(qblocks, block_len, index_width),
        ],
        axis=1,
    )
    columns = jnp.arange(span)
    row_pos = jnp.arange(block_len)
    allowed = (columns[None, :] < picked_count * block_len) | (
        columns[None, :] - picked_count * block_len <= row_pos[:, None]
    )
    local_heads = query_latent.shape[1]
    query_vectors = query_latent.reshape(qblocks, block_len, local_heads, key_width)
    scores = (
        jnp.einsum(
            "cfme,cne->cfmn", query_vectors, latent_key_rows, preferred_element_type=jnp.float32
        )
        * score_scale
    )
    mass_part = attention_mass(scores, allowed[None])
    index_heads = query_index.shape[1]
    indexer_query_rows = query_index.reshape(qblocks, block_len, index_heads, index_width)
    index_head_gains = index_gains.reshape(qblocks, block_len, index_heads)
    inner = jnp.einsum(
        "rtoe,rfe->rtof", indexer_query_rows, indexer_key_rows, preferred_element_type=jnp.float32
    )
    live_heads = jnp.maximum(inner, 0.0)
    logit_portion = jnp.einsum(
        "szc,szco->szo", index_head_gains, live_heads, precision=lax.Precision.HIGHEST
    )
    mass_sum, logits = lax.psum((mass_part, logit_portion), "head")
    divergence, logit_gradient = kl_terms(mass_sum, logits, allowed[None])
    divergence = divergence.reshape(row_count)
    head_gains_gradient = jnp.einsum(
        "nwh,nwgh->nwg", logit_gradient, live_heads, precision=lax.Precision.HIGHEST
    )
    inner_gradient = jnp.where(
        inner > 0, logit_gradient[:, :, None, :] * index_head_gains[:, :, :, None], 0.0
    ).astype(jnp.bfloat16)
    query_grad = jnp.einsum(
        "ecft,ets->ecfs", inner_gradient, indexer_key_rows, preferred_element_type=jnp.float32
    )
    query_grad = query_grad.astype(jnp.bfloat16).reshape(row_count, index_heads, index_width)
    key_grad = jnp.einsum(
        "gnev,gneo->gvo", inner_gradient, indexer_query_rows, preferred_element_type=jnp.float32
    )
    cached_grad = key_grad[:, : picked_count * block_len].reshape(
        slot_count, block_len, index_width
    )
    own_grad = key_grad[:, picked_count * block_len :].reshape(row_count, index_width)
    outgoing = (
        jnp.zeros((seq_count * capacity, block_len, index_width), jnp.float32)
        .at[places]
        .set(cached_grad)
    )
    outgoing = outgoing.reshape(seq_count, capacity, block_len, index_width)
    selector = (wanted[:, None] == jnp.arange(cache_blocks)[None, :]).astype(jnp.float32)
    returned = lax.all_to_all(
        outgoing.astype(jnp.bfloat16), "seq", split_axis=0, concat_axis=0, tiled=True
    ).astype(outgoing.dtype)
    returned = returned.reshape(seq_count * capacity, block_len * index_width)
    cache_grad = jnp.dot(
        selector.T, returned, precision=lax.Precision.HIGHEST, preferred_element_type=jnp.float32
    )
    cache_grad = cache_grad.reshape(cache_blocks * block_len, index_width)
    cache_grad, own_grad = lax.psum((cache_grad, own_grad), "head")
    return (
        divergence,
        query_grad,
        head_gains_gradient.reshape(row_count, index_heads),
        cache_grad,
        own_grad,
    )


def solution(mesh):
    placed = (
        P("seq", "head", None),
        P("seq", None),
        P("seq", None),
        P("seq", "head", None),
        P("seq", None),
        P("seq", None),
        P("seq", "head"),
        P("seq", None),
    )
    return jax.shard_map(
        per_device,
        mesh=mesh,
        in_specs=placed,
        out_specs=(
            P("seq"),
            P("seq", "head", None),
            P("seq", "head"),
            P("seq", None),
            P("seq", None),
        ),
        check_vma=False,
    )
```

profile of v0, /device:TPU:32, one launch (start us, length us, event | category | flops | bytes accessed | tf_op | source)
XLA Modules:
  0.0 390.2 jit_solution(13431445674238135329)
XLA Ops:
  8.5 20.2 %all_to_all.24 = s32[64,1,1]{2,1,0:T(1,128)S(1)} all-to-all(s32[64,1,1]{2,1,0:T(1,128)S(1)} %copy.52), channel_id=1, replica_groups=mesh['seq'=64,'head'=4] {'seq'}, dimensions={0} | all-to-all | bytes 512 | tf_op jit(solution)/shard_map/all_to_all | solution.py:64
  28.7 2.4 fusion.64
  31.1 1.7 gather_fusion.2
  35.1 5.6 %all-to-all-start.2 = ((bf16[64,1,64,128]{3,2,1,0:T(8,128)(2,1)}), bf16[64,1,64,128]{3,2,1,0:T(8,128)(2,1)S(1)}, u32[]{:S(2)}, u32[]{:S(2)}) async-start(bf16[64,1,64,128]{3,2,1,0:T(8,128)(2,1)} %fusion.30), calls=%async_computation.2 | async-start | bytes 2097152 | tf_op jit(solution)/shard_map/all_to_all | solution.py:78
  41.0 3.5 gather_fusion
  44.6 5.7 %fusion.15 = bf16[64,1,64,576]{3,2,1,0:T(8,128)(2,1)} fusion(bf16[64,64,576]{2,1,0:T(8,128)(2,1)} %gather_fusion, pred[64]{0:T(512)(128)(4,1)S(1)} %maximum_compare_fusion, pred[64]{0:T(512)(128)(4,1)S(1)} %compare_reduce_fusion), kind=kLoop, calls=%fused_computation.26 | loop fusion | flops 4718592 | bytes 9437312 | tf_op jit(solution)/shard_map/jit(_where)/select_n | solution.py:72
  50.3 18.5 %all-to-all-done.2 = bf16[64,1,64,128]{3,2,1,0:T(8,128)(2,1)S(1)} async-done(((bf16[64,1,64,128]{3,2,1,0:T(8,128)(2,1)}), bf16[64,1,64,128]{3,2,1,0:T(8,128)(2,1)S(1)}, u32[]{:S(2)}, u32[]{:S(2)}) %all-to-all-start.2) | async-done | bytes 1048608 | tf_op jit(solution)/shard_map/all_to_all | solution.py:78
  68.7 6.7 %all-to-all-start.1 = ((bf16[64,1,64,576]{3,2,1,0:T(8,128)(2,1)}), bf16[64,1,64,576]{3,2,1,0:T(8,128)(2,1)}, u32[]{:S(2)}, u32[]{:S(2)}) async-start(bf16[64,1,64,576]{3,2,1,0:T(8,128)(2,1)} %fusion.15), calls=%async_computation.1 | async-start | bytes 10485760 | tf_op jit(solution)/shard_map/all_to_all | solution.py:77
  76.1 16.7 %copy.58 = bf16[256,32,576]{2,1,0:T(8,128)(2,1)} copy(bf16[256,32,576]{0,2,1:T(8,128)(2,1)} %param.8) | data formatting | bytes 18874368 | tf_op args[0]
  96.4 1.8 maximum_bitcast_fusion
  98.2 2.6 copy-done.2
  100.8 3.3 copy-done.1
  104.0 8.0 %fusion.12 = f32[4,64,1,512]{3,2,1,0:T(1,128)S(1)} fusion(f32[4,64,16,1]{2,3,1,0:T(1,128)S(1)} %bitcast.98, f32[4,64,16,512]{3,1,2,0:T(8,128)S(1)} %maximum_bitcast_fusion), kind=kOutput, calls=%fused_computation.22 | convolution fusion | flops 25165824 | bytes 8929280 | tf_op jit(solution)/shard_map/szc,szco->szo/dot_general | solution.py:121
  112.9 80.3 %all-to-all-done.1 = bf16[64,1,64,576]{3,2,1,0:T(8,128)(2,1)} async-done(((bf16[64,1,64,576]{3,2,1,0:T(8,128)(2,1)}), bf16[64,1,64,576]{3,2,1,0:T(8,128)(2,1)}, u32[]{:S(2)}, u32[]{:S(2)}) %all-to-all-start.1) | async-done | bytes 4718624 | tf_op jit(solution)/shard_map/all_to_all | solution.py:77
  193.2 4.8 %gather_fusion.1 = bf16[28,64,576]{2,1,0:T(8,128)(2,1)} fusion(bf16[64,64,576]{2,1,0:T(8,128)(2,1)} %bitcast.4, s32[1024]{0:T(1024)S(1)} %pad_clamp_fusion), kind=kCustom, calls=%fused_computation.1 | custom fusion | bytes 4128880 | tf_op jit(solution)/shard_map/jit(_take)/gather | solution.py:80
  198.0 2.9 copy.55
  201.1 13.2 %fusion.5 = f32[4,512,64,32]{1,2,3,0:T(8,128)} fusion(bf16[4,64,32,576]{3,2,1,0:T(8,128)(2,1)} %bitcast.88, bf16[4,64,576]{1,2,0:T(8,128)(2,1)} %copy.57, bf16[4,448,576]{1,2,0:T(8,128)(2,1)S(1)} %broadcast_select_fusion), kind=kOutput, calls=%fused_computation.13 | convolution fusion | flops 4836556800 | bytes 28573696 | tf_op jit(solution)/shard_map/cfme,cne->cfmn/dot_general | solution.py:108
  214.3 18.8 %divide_reduce_fusion = f32[4,64,512]{2,1,0:T(8,128)} fusion(f32[4,512,64,32]{1,2,3,0:T(8,128)} %fusion.5, pred[64,512]{1,0:T(8,128)(4,1)S(1)} %fusion.44), kind=kOutput, calls=%fused_computation.11 | output fusion | flops 29246464 | bytes 17334272 | tf_op jit(solution)/shard_map/div | solution.py:16
  233.2 48.3 %all-reduce.7.cloned.1.call-done = (f32[4,64,512]{2,1,0:T(8,128)}, f32[4,64,512]{2,1,0:T(8,128)}) async-done(((f32[4,64,512]{2,1,0:T(8,128)}, f32[4,64,512]{2,1,0:T(8,128)}), (f32[4,64,512]{2,1,0:T(8,128)}, f32[4,64,512]{2,1,0:T(8,128)})) %all-reduce.7.cloned.1.call-update) | async-done | bytes 1048592 | tf_op jit(solution)/shard_map/psum | solution.py:124
  281.5 1.5 fusion.26
  283.0 4.2 %select_convert_fusion = bf16[4,64,16,512]{3,1,2,0:T(8,128)(2,1)S(1)} fusion(f32[4,512,64,16]{1,2,3,0:T(8,128)} %copy-done.2, f32[4,64,16]{1,2,0:T(8,128)S(1)} %copy.61, f32[4,64,512]{2,1,0:T(8,128)S(1)} %fusion.26), kind=kLoop, calls=%fused_computation.15 | loop fusion | flops 8388608 | bytes 13123584 | tf_op jit(solution)/shard_map/convert_element_type | solution.py:132
  287.2 1.7 convolution_bitcast_fusion
  290.7 3.5 scatter_fusion
  295.4 10.5 %all-to-all-start.3 = ((bf16[64,1,64,128]{3,2,1,0:T(8,128)(2,1)}), bf16[64,1,64,128]{3,2,1,0:T(8,128)(2,1)S(1)}, u32[]{:S(2)}, u32[]{:S(2)}) async-start(bf16[64,1,64,128]{3,2,1,0:T(8,128)(2,1)} %convert_bitcast_fusion), calls=%async_computation.3 | async-start | bytes 2097152 | tf_op jit(solution)/shard_map/all_to_all | solution.py:151
  305.9 1.6 slice.17
  307.6 15.1 %fusion.10 = f32[4,64,1,16]{3,2,1,0:T(1,128)S(1)} fusion(f32[4,64,16,512]{3,1,2,0:T(8,128)} %copy-done.1, f32[4,64,512,1]{2,1,0,3:T(8,128)} %bitcast.94), kind=kOutput, calls=%fused_computation.20 | convolution fusion | flops 25165824 | bytes 8929280 | tf_op jit(solution)/shard_map/nwh,nwgh->nwg/dot_general | solution.py:127
  323.5 1.3 exponential_reduce_fusion
  325.8 8.0 %all-to-all-done.3 = bf16[64,1,64,128]{3,2,1,0:T(8,128)(2,1)S(1)} async-done(((bf16[64,1,64,128]{3,2,1,0:T(8,128)(2,1)}), bf16[64,1,64,128]{3,2,1,0:T(8,128)(2,1)S(1)}, u32[]{:S(2)}, u32[]{:S(2)}) %all-to-all-start.3) | async-done | bytes 1048608 | tf_op jit(solution)/shard_map/all_to_all | solution.py:151
  335.3 5.6 %fusion.20 = bf16[4,64,16,128]{3,2,1,0:T(8,128)(2,1)} fusion(bf16[4,64,16,512]{3,1,2,0:T(8,128)(2,1)} %copy-done.3, bf16[4,64,128]{2,1,0:T(8,128)(2,1)S(1)} %bitcast.102, bf16[4,448,128]{2,1,0:T(8,128)(2,1)S(1)} %copy-done.6), kind=kOutput, calls=%fused_computation.34 | convolution fusion | flops 538443776 | bytes 5767168 | tf_op jit(solution)/shard_map/ecft,ets->ecfs/dot_general | solution.py:133
  340.9 38.8 %all-reduce.5.cloned.1.call-done = (f32[512,128]{1,0:T(8,128)}, f32[256,128]{1,0:T(8,128)}) async-done(((f32[512,128]{1,0:T(8,128)}, f32[256,128]{1,0:T(8,128)}), (f32[512,128]{1,0:T(8,128)}, f32[256,128]{1,0:T(8,128)})) %all-reduce.5.cloned.1.call-update) | async-done | bytes 393232 | tf_op jit(solution)/shard_map/psum | solution.py:159
  379.7 1.7 copy.101
  381.4 1.6 copy.102
  (72 shorter events, 15.7 us)
Async XLA Ops:
  7.2 87.9 %copy-start = (bf16[256,16,128]{2,1,0:T(8,128)(2,1)S(1)}, bf16[256,16,128]{2,1,0:T(8,128)(2,1)}, u32[]{:S(2)}) copy-start(bf16[256,16,128]{2,1,0:T(8,128)(2,1)} %param.11) | copy-start | bytes 3145732
  7.2 33.5 %copy-start.8 = (bf16[512,576]{0,1:T(8,128)(2,1)S(1)}, bf16[512,576]{0,1:T(8,128)(2,1)}, u32[]{:S(2)}) copy-start(bf16[512,576]{0,1:T(8,128)(2,1)} %param.10) | copy-start | bytes 1769476
  35.1 33.6 %all-to-all-start.2 = ((bf16[64,1,64,128]{3,2,1,0:T(8,128)(2,1)}), bf16[64,1,64,128]{3,2,1,0:T(8,128)(2,1)S(1)}, u32[]{:S(2)}, u32[]{:S(2)}) async-start(bf16[64,1,64,128]{3,2,1,0:T(8,128)(2,1)} %fusion.30), calls=%async_computation.2 | async-start | bytes 2097152 | tf_op jit(solution)/shard_map/all_to_all | solution.py:78
  50.2 25.4 %copy-start.13 = (s32[4,7]{1,0:T(4,128)S(1)}, s32[4,7]{1,0:T(4,128)}, u32[]{:S(2)}) copy-start(s32[4,7]{1,0:T(4,128)} %param.15) | copy-start | bytes 340
  50.2 25.8 %copy-start.12 = (f32[256,16]{0,1:T(8,128)S(1)}, f32[256,16]{0,1:T(8,128)}, u32[]{:S(2)}) copy-start(f32[256,16]{0,1:T(8,128)} %param.14) | copy-start | bytes 49156
  68.7 124.5 %all-to-all-start.1 = ((bf16[64,1,64,576]{3,2,1,0:T(8,128)(2,1)}), bf16[64,1,64,576]{3,2,1,0:T(8,128)(2,1)}, u32[]{:S(2)}, u32[]{:S(2)}) async-start(bf16[64,1,64,576]{3,2,1,0:T(8,128)(2,1)} %fusion.15), calls=%async_computation.1 | async-start | bytes 10485760 | tf_op jit(solution)/shard_map/all_to_all | solution.py:77
  75.4 206.0 %all-reduce.7.cloned.1.call-start = ((), (), s32[]{:S(2)}) async-start(), calls=%async_computation.5 | async-start | bytes 2097152 | tf_op jit(solution)/shard_map/psum | solution.py:124
  76.1 16.7 %copy-start.10 = (bf16[256,576]{0,1:T(8,128)(2,1)S(1)}, bf16[256,576]{0,1:T(8,128)(2,1)}, u32[]{:S(2)}) copy-start(bf16[256,576]{0,1:T(8,128)(2,1)} %param.9) | copy-start | bytes 884740
  76.1 19.0 %copy-start.11 = (bf16[256,128]{1,0:T(8,128)(2,1)S(1)}, bf16[256,128]{1,0:T(8,128)(2,1)}, u32[]{:S(2)}) copy-start(bf16[256,128]{1,0:T(8,128)(2,1)} %param.12) | copy-start | bytes 196612
  95.1 3.1 copy-start.5
  96.4 4.4 %copy-start.2 = (f32[4,512,64,16]{1,2,3,0:T(8,128)}, f32[4,512,64,16]{1,2,3,0:T(8,128)S(1)}, u32[]{:S(2)}) copy-start(f32[4,512,64,16]{1,2,3,0:T(8,128)S(1)} %fusion.32) | copy-start | bytes 25165828
  100.8 3.3 copy-start.1
  282.9 4.2 %copy-start.4 = (f32[4,64,512]{2,1,0:T(8,128)}, f32[4,64,512]{2,1,0:T(8,128)S(1)}, u32[]{:S(2)}) copy-start(f32[4,64,512]{2,1,0:T(8,128)S(1)} %fusion.26) | copy-start | bytes 1572868
  287.2 1.9 copy-start.3
  289.1 1.3 copy-start.7
  295.4 38.4 %all-to-all-start.3 = ((bf16[64,1,64,128]{3,2,1,0:T(8,128)(2,1)}), bf16[64,1,64,128]{3,2,1,0:T(8,128)(2,1)S(1)}, u32[]{:S(2)}, u32[]{:S(2)}) async-start(bf16[64,1,64,128]{3,2,1,0:T(8,128)(2,1)} %convert_bitcast_fusion), calls=%async_computation.3 | async-start | bytes 2097152 | tf_op jit(solution)/shard_map/all_to_all | solution.py:151
  305.9 18.9 %copy-start.9 = (f32[4,64,512]{2,1,0:T(8,128)S(1)}, f32[4,64,512]{2,1,0:T(8,128)}, u32[]{:S(2)}) copy-start(f32[4,64,512]{2,1,0:T(8,128)} %get-tuple-element.10) | copy-start | bytes 1572868
  305.9 73.8 %all-reduce.5.cloned.1.call-start = ((), (), s32[]{:S(2)}) async-start(), calls=%async_computation.4 | async-start | bytes 786432 | tf_op jit(solution)/shard_map/psum | solution.py:159
  307.6 27.7 %copy-start.6 = (bf16[4,448,128]{2,1,0:T(8,128)(2,1)S(1)}, bf16[4,448,128]{2,1,0:T(8,128)(2,1)}, u32[]{:S(2)}) copy-start(bf16[4,448,128]{2,1,0:T(8,128)(2,1)} %copy-done.5) | copy-start | bytes 1376260
Sparse Core Ops, SparseCore 0:
  233.2 48.1 all-reduce.6
  335.4 44.2 all-reduce.4
where the time goes:
time: 397 us; the launch traced here: 390 us
  waiting for transfers between devices  194 us (49%)
  local copies, waits for them, and re-layouts  52.3 us (13%)
  matrix products  45.6 us (11%)
  other arithmetic  40.5 us (10%)
  starting transfers between devices  23 us (6%)
  blocking collectives  20.2 us (5%)
  between operations  14.8 us (4%)
    all_to_all x1, waiting for transfers between devices, per_device(): lax.all_to_all(served_latent, 'seq', split_axis=0, concat_axis=0, tiled=T...  80.3 us
    psum x1, waiting for transfers between devices, per_device(): mass_sum, logits = lax.psum((mass_part, logit_portion), 'head')  48.3 us
    psum x1, waiting for transfers between devices, per_device(): cache_grad, own_grad = lax.psum((cache_grad, own_grad), 'head')  38.8 us
    unnamed x33, local copies, waits for them, and re-layouts  26.8 us
    all_to_all x1, blocking collectives, per_device(): lax.all_to_all(request.reshape(seq_count, capacity), 'seq', split_axis=0,...  20.2 us
    div x1, other arithmetic, attention_mass(): attention = shifted / jnp.sum(shifted, axis=-1, keepdims=True)  18.8 us
    all_to_all x1, waiting for transfers between devices, per_device(): lax.all_to_all(served_index, 'seq', split_axis=0, concat_axis=0, tiled=True)  18.5 us
    dot_general x1, matrix products, per_device(): jnp.einsum('nwh,nwgh->nwg', logit_gradient, live_heads, precision=lax.Pre...  15.1 us
  transfers between devices with their start and end apart: 5, of which 5 were waited for; matrix products, arithmetic and copies ran while one was open for 17% of the time, Pallas kernels for 0%

commit v1 on v0

v1 whole, which is shorter than its diff:
```python
import functools

import jax
import jax.numpy as jnp
from jax import lax
from jax.experimental import pallas as pl
from jax.experimental.pallas import tpu as pltpu
from jax.sharding import PartitionSpec as P

MESH = pl.DeviceIdType.MESH
HEADS = 128
SCORE_SCALE = 192.0 ** (-0.5)
LOG2E = 1.4426950408889634
BLK = 64
PICKED = 7
QBLK = 4
NX = 4
NZ = 8
NP = 8
QROWS = BLK // NX
KDIM = 576
IDIM = 128
SPAN = 512


def z_place(offset):
    return jnp.where(offset == 0, 0, jnp.where(offset <= 4, 2 * offset - 1, 2 * (8 - offset)))


def place_offset(place):
    return jnp.where(place % 2 == 1, (place + 1) // 2, NZ - place // 2)


def gather_kernel(
    ids,
    cl,
    ci,
    sl,
    si,
    out_latent,
    out_index,
    out_want,
    *scratch,
):
    stock_l, stock_i = scratch[:NZ], scratch[NZ : 2 * NZ]
    send_l, send_i, recv_l, recv_i, key_l, key_i, want_v, want_s = scratch[2 * NZ : 2 * NZ + 8]
    local_sem, ids_send, ids_recv, z_send, z_recv, y_send, y_recv, x_send, x_recv = scratch[
        2 * NZ + 8 :
    ]
    seq = lax.axis_index("seq")
    h = lax.axis_index("head")
    z, me = seq // NP, seq % NP
    z_next, z_prev = ((z + 1) % NZ) * NP + me, ((z + NZ - 1) % NZ) * NP + me
    x_next, x_prev = (h + 1) % NX, (h + NX - 1) % NX

    loads = [
        pltpu.make_async_copy(cl.at[:, h], stock_l[0], local_sem.at[0]),
        pltpu.make_async_copy(ci.at[:, h], stock_i[0], local_sem.at[1]),
        pltpu.make_async_copy(sl, key_l.at[:, PICKED], local_sem.at[2]),
        pltpu.make_async_copy(si, key_i.at[:, PICKED], local_sem.at[3]),
    ]
    for load in loads:
        load.start()

    barrier = pltpu.get_barrier_semaphore()
    for target in ((z_next, h), (z_prev, h), (seq, x_next), (seq, x_prev)):
        pl.semaphore_signal(barrier, inc=1, device_id=target, device_id_type=MESH)

    def greet(i, _):
        pl.semaphore_signal(
            barrier, inc=1, device_id=(z * NP + (me + i) % NP, h), device_id_type=MESH
        )
        return 0

    lax.fori_loop(1, NP, greet, 0)

    lane = lax.broadcasted_iota(jnp.int32, (8, 128), 1)
    row = lax.broadcasted_iota(jnp.int32, (8, 128), 0)
    tile = jnp.full((8, 128), -1, jnp.int32)
    for r in range(QBLK):
        for j in range(PICKED):
            block = ids[r, j]
            owner = block >> 3
            spot = (owner & 7) * NZ + z_place(((owner >> 3) - z + NZ) & 7)
            value = jnp.where(row == 0, block & 7, r * 8 + j)
            tile = jnp.where(lane == spot, value, tile)
    want_v[me] = tile

    pl.semaphore_wait(barrier, 4 + NP - 1)

    def ids_copy(i):
        peer = (me + i) % NP
        return pltpu.make_async_remote_copy(
            src_ref=want_v.at[me],
            dst_ref=want_v.at[me],
            send_sem=ids_send.at[i],
            recv_sem=ids_recv.at[i],
            device_id=(z * NP + peer, h),
            device_id_type=MESH,
        )

    def ids_start(i, _):
        ids_copy(i).start()
        return 0

    lax.fori_loop(1, NP, ids_start, 0)

    def z_copies(step, way):
        if way == 0:
            src, dst = 2 * (step - 1), 2 * step if step < 4 else 7
            part, target = pl.ds(0, 4), z_next
        else:
            src, dst = max(2 * step - 3, 0), 2 * step - 1
            part, target = pl.ds(4, 4), z_prev
        if step < 4:
            part = pl.ds(0, 8)
        return [
            pltpu.make_async_remote_copy(
                src_ref=stock[src].at[part],
                dst_ref=stock[dst].at[part],
                send_sem=z_send.at[a, way, step],
                recv_sem=z_recv.at[a, way, step],
                device_id=(target, h),
                device_id_type=MESH,
            )
            for a, stock in enumerate((stock_l, stock_i))
        ]

    loads[0].wait()
    loads[1].wait()
    for way in range(2):
        for copy in z_copies(1, way):
            copy.start()

    def ids_wait(i, _):
        ids_copy(i).wait()
        return 0

    lax.fori_loop(1, NP, ids_wait, 0)
    to_scalar = pltpu.make_async_copy(want_v, want_s, local_sem.at[4])
    to_scalar.start()
    to_scalar.wait()

    def y_copies(i, step, first, count):
        peer = (me + i) % NP
        return [
            pltpu.make_async_remote_copy(
                src_ref=send.at[peer, pl.ds(first, count)],
                dst_ref=recv.at[me, pl.ds(first, count)],
                send_sem=y_send.at[a, step, i],
                recv_sem=y_recv.at[a, step, i],
                device_id=(z * NP + peer, h),
                device_id_type=MESH,
            )
            for a, (send, recv) in enumerate(((send_l, recv_l), (send_i, recv_i)))
        ]

    spans = ((0, 1), (1, 2), (3, 2), (5, 2), (7, 1))
    for step, (first, count) in enumerate(spans):
        if step:
            for way in range(2):
                for copy in z_copies(step, way):
                    copy.wait_recv()
            if step < 4:
                for way in range(2):
                    for copy in z_copies(step + 1, way):
                        copy.start()

        def stage(i, _, step=step, first=first, count=count):
            peer = (me + i) % NP
            for q in range(first, first + count):
                block = jnp.maximum(want_s[peer, 0, me * NZ + q], 0)
                send_l[peer, q] = stock_l[q][block]
                send_i[peer, q] = stock_i[q][block]
            for copy in y_copies(i, step, first, count):
                copy.start()
            return 0

        lax.fori_loop(1, NP, stage, 0)
        for q in range(first, first + count):
            block = jnp.maximum(want_s[me, 0, me * NZ + q], 0)
            recv_l[me, q] = stock_l[q][block]
            recv_i[me, q] = stock_i[q][block]

    for step, (first, count) in enumerate(spans):

        def y_wait(i, _, step=step, first=first, count=count):
            for copy in y_copies(i, step, first, count):
                copy.wait()
            return 0

        lax.fori_loop(1, NP, y_wait, 0)

    def x_copies(r, step, way):
        if step == 0:
            quarter, part = h, pl.ds(0, PICKED)
        elif way == 0:
            quarter, part = x_prev, pl.ds(0, 4)
        else:
            quarter, part = x_next, pl.ds(4, 3)
        return [
            pltpu.make_async_remote_copy(
                src_ref=key.at[r, part, quarter],
                dst_ref=key.at[r, part, quarter],
                send_sem=x_send.at[a, r, step, way],
                recv_sem=x_recv.at[a, r, step, way],
                device_id=(seq, x_prev if way else x_next),
                device_id_type=MESH,
            )
            for a, key in enumerate((key_l, key_i))
        ]

    for r in range(QBLK):
        for j in range(PICKED):
            owner = ids[r, j] >> 3
            place = z_place(((owner >> 3) - z + NZ) & 7)
            key_l[r, j, h] = recv_l[owner & 7, place]
            key_i[r, j, h] = recv_i[owner & 7, place]
        for way in range(2):
            for copy in x_copies(r, 0, way):
                copy.start()
    for r in range(QBLK):
        for way in range(2):
            for copy in x_copies(r, 0, way):
                copy.wait_recv()
        for way in range(2):
            for copy in x_copies(r, 1, way):
                copy.start()
    loads[2].wait()
    loads[3].wait()
    stores = []
    for r in range(QBLK):
        for way in range(2):
            for copy in x_copies(r, 1, way):
                copy.wait_recv()
        for a, (key, out) in enumerate(((key_l, out_latent), (key_i, out_index))):
            store = pltpu.make_async_copy(key.at[r], out.at[r], local_sem.at[5 + 2 * r + a])
            store.start()
            stores.append(store)
    store = pltpu.make_async_copy(want_v, out_want, local_sem.at[13])
    store.start()
    stores.append(store)
    for r in range(QBLK):
        for step in range(2):
            for way in range(2):
                for copy in x_copies(r, step, way):
                    copy.wait_send()
    for step in range(1, 5):
        for way in range(2):
            for copy in z_copies(step, way):
                copy.wait_send()
    for store in stores:
        store.wait()


def gather_keys(block_ids, cache_latent, cache_index, stretch_latent, stretch_index):
    bf16, sem = jnp.bfloat16, pltpu.SemaphoreType.DMA
    any_space = pl.BlockSpec(memory_space=pl.ANY)
    return pl.pallas_call(
        gather_kernel,
        out_shape=(
            jax.ShapeDtypeStruct((QBLK, 8, NX, QROWS, KDIM), bf16),
            jax.ShapeDtypeStruct((QBLK, 8, NX, QROWS, IDIM), bf16),
            jax.ShapeDtypeStruct((NP, 8, 128), jnp.int32),
        ),
        in_specs=[pl.BlockSpec(memory_space=pltpu.SMEM)] + [any_space] * 4,
        out_specs=(any_space,) * 3,
        scratch_shapes=[
            *[pltpu.VMEM((8, QROWS, KDIM), bf16)] * NZ,
            *[pltpu.VMEM((8, QROWS, IDIM), bf16)] * NZ,
            pltpu.VMEM((NP, NZ, QROWS, KDIM), bf16),
            pltpu.VMEM((NP, NZ, QROWS, IDIM), bf16),
            pltpu.VMEM((NP, NZ, QROWS, KDIM), bf16),
            pltpu.VMEM((NP, NZ, QROWS, IDIM), bf16),
            pltpu.VMEM((QBLK, 8, NX, QROWS, KDIM), bf16),
            pltpu.VMEM((QBLK, 8, NX, QROWS, IDIM), bf16),
            pltpu.VMEM((NP, 8, 128), jnp.int32),
            pltpu.SMEM((NP, 8, 128), jnp.int32),
            sem((14,)),
            sem((NP,)),
            sem((NP,)),
            sem((2, 2, 5)),
            sem((2, 2, 5)),
            sem((2, 5, NP)),
            sem((2, 5, NP)),
            sem((2, QBLK, 2, 2)),
            sem((2, QBLK, 2, 2)),
        ],
        compiler_params=pltpu.CompilerParams(
            collective_id=0, has_side_effects=True, vmem_limit_bytes=40 << 20
        ),
        name="gather_keys",
    )(
        block_ids,
        cache_latent.reshape(8, NX, QROWS, KDIM),
        cache_index.reshape(8, NX, QROWS, IDIM),
        stretch_latent.reshape(QBLK, NX, QROWS, KDIM),
        stretch_index.reshape(QBLK, NX, QROWS, IDIM),
    )


QUAD = 4
PART = 16


def forward_kernel(q, key_l, key_i, qi, gains, mass, logits, sums):
    step = pl.program_id(1)
    iheads = qi.shape[1]
    row = lax.broadcasted_iota(jnp.int32, (BLK, QUAD * BLK), 0)
    token = lax.broadcasted_iota(jnp.int32, (BLK, QUAD * BLK), 1) % BLK
    allowed = row <= token
    cut = PICKED * BLK
    scale = SCORE_SCALE * LOG2E
    for r in range(2):
        keys = key_l[r].reshape(SPAN, KDIM)
        queries = jnp.concatenate([q[i, :, r * BLK : (r + 1) * BLK] for i in range(QUAD)], axis=1)
        scores = jnp.dot(keys, queries, preferred_element_type=jnp.float32)
        old, own = scores[:cut], jnp.where(allowed, scores[cut:], -jnp.inf)
        top = jnp.maximum(jnp.max(old, axis=0, keepdims=True), jnp.max(own, axis=0, keepdims=True))
        e_old = jnp.exp2((old - top) * scale)
        e_own = jnp.exp2((own - top) * scale)
        total = jnp.sum(e_old, axis=0, keepdims=True) + jnp.sum(e_own, axis=0, keepdims=True)
        share = 1.0 / total

        @pl.when(step == 0)
        def _():
            sums[r, :cut] = e_old * share
            sums[r, cut:] = e_own * share

        @pl.when(step > 0)
        def _():
            sums[r, :cut] += e_old * share
            sums[r, cut:] += e_own * share

    ikeys = key_i[step // 4].reshape(SPAN, IDIM)
    tokens = pl.ds(pl.multiple_of(step * PART, PART), PART)
    iblock = qi[tokens].reshape(PART * iheads, IDIM)
    inner = lax.dot_general(
        iblock, ikeys, (((1,), (1,)), ((), ())), preferred_element_type=jnp.float32
    )
    gain = pltpu.roll(gains[...], 2 * BLK - step * PART, 1)
    rows = []
    for t in range(PART):
        live = jnp.maximum(inner[t * iheads : (t + 1) * iheads], 0.0)
        rows.append(jnp.sum(live * gain[:, t : t + 1], axis=0, keepdims=True))
    logits[tokens] = jnp.concatenate(rows, axis=0)

    @pl.when(step == pl.num_programs(1) - 1)
    def _():
        for r in range(2):
            pair = sums[r, :, : 2 * BLK] + sums[r, :, 2 * BLK :]
            mass[pl.ds(r * BLK, BLK)] = (pair[:, :BLK] + pair[:, BLK:]).T


def forward(query_latent, key_l, key_i, query_index, index_gains):
    rows, heads, _ = query_latent.shape
    iheads = query_index.shape[1]
    whole = lambda p, s: (p, 0, 0, 0, 0)
    return pl.pallas_call(
        forward_kernel,
        grid=(QBLK // 2, heads // QUAD),
        in_specs=[
            pl.BlockSpec((QUAD, KDIM, 2 * BLK), lambda p, s: (s, 0, p)),
            pl.BlockSpec((2, 8, NX, QROWS, KDIM), whole),
            pl.BlockSpec((2, 8, NX, QROWS, IDIM), whole),
            pl.BlockSpec((2 * BLK, iheads, IDIM), lambda p, s: (p, 0, 0)),
            pl.BlockSpec((iheads, 2 * BLK), lambda p, s: (0, p)),
        ],
        out_specs=[pl.BlockSpec((2 * BLK, SPAN), lambda p, s: (p, 0))] * 2,
        out_shape=[jax.ShapeDtypeStruct((rows, SPAN), jnp.float32)] * 2,
        scratch_shapes=[pltpu.VMEM((2, SPAN, QUAD * BLK), jnp.float32)],
        compiler_params=pltpu.CompilerParams(vmem_limit_bytes=48 << 20),
        name="forward",
    )(
        jnp.transpose(query_latent, (1, 2, 0)),
        key_l,
        key_i,
        query_index,
        index_gains.T,
    )


BCHUNK = 16


def backward_kernel(
    mass,
    logits,
    qi,
    gains,
    key_i,
    want,
    out_div,
    out_qgrad,
    out_ggrad,
    out_cache,
    out_own,
    mass_b,
    rs_m,
    rs_l,
    lg,
    div,
    kgrad,
    kquarter,
    kpart,
    krecv,
    slots,
    ret_s,
    ret_r,
    z_part,
    z_got,
    cache_g,
    own_g,
    out_sem,
    rs_send,
    rs_recv,
    lg_send,
    lg_recv,
    k_send,
    k_recv,
    y_send,
    y_recv,
    z_send,
    z_recv,
    f_send,
    f_recv,
    ggrad_t,
):
    seq = lax.axis_index("seq")
    h = lax.axis_index("head")
    z, me = seq // NP, seq % NP
    iheads = qi.shape[1]

    barrier = pltpu.get_barrier_semaphore()

    def greet_x(i, _):
        pl.semaphore_signal(
            barrier, inc=1, device_id=(seq, (h + i) % NX), device_id_type=MESH
        )
        return 0

    def greet_y(i, _):
        pl.semaphore_signal(
            barrier, inc=1, device_id=(z * NP + (me + i) % NP, h), device_id_type=MESH
        )
        return 0

    def greet_z(i, _):
        pl.semaphore_signal(
            barrier, inc=1, device_id=(((z + i) % NZ) * NP + me, h), device_id_type=MESH
        )
        return 0

    lax.fori_loop(1, NX, greet_x, 0)
    lax.fori_loop(1, NP, greet_y, 0)
    lax.fori_loop(1, NZ, greet_z, 0)
    for r in range(QBLK):
        mass_b[r] = mass[r].astype(jnp.bfloat16)
    pl.semaphore_wait(barrier, NX - 1 + NP - 1 + NZ - 1)

    def remote(src, dst, send, recv, target):
        return pltpu.make_async_remote_copy(
            src_ref=src,
            dst_ref=dst,
            send_sem=send,
            recv_sem=recv,
            device_id=target,
            device_id_type=MESH,
        )

    def each(count, copies, act):
        def body(i, _):
            for copy in copies(i):
                act(copy)
            return 0

        lax.fori_loop(1, count, body, 0)

    start = lambda copy: copy.start()
    wait = lambda copy: copy.wait()
    wait_recv = lambda copy: copy.wait_recv()
    wait_send = lambda copy: copy.wait_send()

    def rs_copies(i):
        peer = (h + i) % NX
        return [
            remote(mass_b.at[peer], rs_m.at[h], rs_send.at[0, i], rs_recv.at[0, i], (seq, peer)),
            remote(logits.at[peer], rs_l.at[h], rs_send.at[1, i], rs_recv.at[1, i], (seq, peer)),
        ]

    each(NX, rs_copies, start)
    each(NX, rs_copies, wait)
    mass_sum, logit = mass[h], logits[h]
    for i in range(1, NX):
        mass_sum = mass_sum + rs_m[(h + i) % NX].astype(jnp.float32)
        logit = logit + rs_l[(h + i) % NX]
    target = mass_sum * (1.0 / HEADS)
    column = lax.broadcasted_iota(jnp.int32, (BLK, SPAN), 1)
    token = lax.broadcasted_iota(jnp.int32, (BLK, SPAN), 0)
    allowed = column - PICKED * BLK <= token
    masked = jnp.where(allowed, logit, -jnp.inf)
    shifted = masked - jnp.max(masked, axis=1, keepdims=True)
    powers = jnp.exp(shifted)
    total = jnp.sum(powers, axis=1, keepdims=True)
    model = powers / total
    log_model = jnp.where(allowed, shifted - jnp.log(total), 0.0)
    safe = jnp.where(target > 0, target, 1.0)
    pointwise = jnp.where(allowed, target * (jnp.log(safe) - log_model), 0.0)
    divergence = jnp.sum(pointwise, axis=1, keepdims=True)
    lg[h] = jnp.where(allowed, model - target, 0.0).astype(jnp.bfloat16)
    diagonal = lax.broadcasted_iota(jnp.int32, (BLK, 128), 0) == lax.broadcasted_iota(
        jnp.int32, (BLK, 128), 1
    )
    in_lanes = jnp.sum(jnp.where(diagonal, divergence, 0.0), axis=0, keepdims=True)
    div[h] = jnp.broadcast_to(in_lanes, (8, 128))

    def lg_copies(i):
        peer = (h + i) % NX
        return [
            remote(lg.at[h], lg.at[h], lg_send.at[0, i], lg_recv.at[0, i], (seq, peer)),
            remote(div.at[h], div.at[h], lg_send.at[1, i], lg_recv.at[1, i], (seq, peer)),
        ]

    each(NX, lg_copies, start)

    def k_copy(i, r):
        peer = (h + i) % NX
        return remote(
            kpart.at[r, :, peer], krecv.at[h, r], k_send.at[i, r], k_recv.at[i, r], (seq, peer)
        )

    def backward(d, _):
        r = (h + NX - d) % NX

        @pl.when(d > 0)
        def _():
            for copy in lg_copies(d):
                copy.wait_recv()

        ikeys = key_i[r].reshape(SPAN, IDIM)
        kgrad[...] = jnp.zeros_like(kgrad)

        def part(c, _):
            first = pl.multiple_of(c * BCHUNK, BCHUNK)
            rows = pl.ds(r * BLK + first, BCHUNK)
            iblock = qi[rows].reshape(BCHUNK * iheads, IDIM)
            inner = lax.dot_general(
                iblock, ikeys, (((1,), (1,)), ((), ())), preferred_element_type=jnp.float32
            )
            slope = lg[r, pl.ds(first, BCHUNK)].astype(jnp.float32)
            start_lane = (r % 2) * BLK + first
            gain = pltpu.roll(gains[:, pl.ds(pl.multiple_of((r // 2) * 128, 128), 128)], 128 - start_lane, 1)
            lane = lax.broadcasted_iota(jnp.int32, (iheads, 128), 1)
            found = jnp.zeros((iheads, 128), jnp.float32)
            grads = []
            for t in range(BCHUNK):
                piece = inner[t * iheads : (t + 1) * iheads]
                push = slope[t : t + 1]
                gsum = jnp.sum(jnp.maximum(piece, 0.0) * push, axis=1, keepdims=True)
                found = jnp.where(lane == start_lane + t, gsum, found)
                grads.append(
                    jnp.where(piece > 0, push * gain[:, t : t + 1], 0.0).astype(jnp.bfloat16)
                )
            ggrad_t[r // 2] += found
            inner_grad = jnp.concatenate(grads, axis=0)
            qgrad = jnp.dot(inner_grad, ikeys, preferred_element_type=jnp.float32)
            out_qgrad[rows] = qgrad.astype(jnp.bfloat16).reshape(BCHUNK, iheads, IDIM)
            kgrad[...] += lax.dot_general(
                inner_grad, iblock, (((0,), (0,)), ((), ())), preferred_element_type=jnp.float32
            )
            return 0

        lax.fori_loop(0, BLK // BCHUNK, part, 0)
        for j in range(8):
            block = kgrad[pl.ds(j * BLK, BLK)].reshape(NX, QROWS, IDIM)
            kpart[r, j] = block.astype(jnp.bfloat16)
            kquarter[r, j] = kgrad[pl.ds(j * BLK + h * QROWS, QROWS)]

        def send(i, _):
            k_copy(i, r).start()
            return 0

        lax.fori_loop(1, NX, send, 0)
        return 0

    ggrad_t[...] = jnp.zeros_like(ggrad_t)
    lax.fori_loop(0, NX, backward, 0)
    out_ggrad[:, :128] = ggrad_t[0]
    out_ggrad[:, 128:] = ggrad_t[1]

    for r in range(QBLK):

        def k_wait(i, _, r=r):
            k_copy(i, r).wait()
            return 0

        lax.fori_loop(1, NX, k_wait, 0)
        total = kquarter[r]
        for i in range(1, NX):
            total = total + krecv[(h + i) % NX, r].astype(jnp.float32)
        own_g[r, h] = total[PICKED]
        slots[pl.ds(r * 8, 8)] = total.astype(jnp.bfloat16)

    def put_back(p, _):
        for q in range(NZ):
            slot = jnp.maximum(want[me, 1, p * NZ + q], 0)
            ret_s[p, q] = slots[slot]
        return 0

    lax.fori_loop(0, NP, put_back, 0)

    def y_copies(i):
        peer = (me + i) % NP
        return [
            remote(ret_s.at[peer], ret_r.at[me], y_send.at[i], y_recv.at[i], (z * NP + peer, h))
        ]

    each(NP, y_copies, start)

    def own_copies(i):
        peer = (h + i) % NX
        return [remote(own_g.at[:, h], own_g.at[:, h], f_send.at[0, i], f_recv.at[0, i], (seq, peer))]

    each(NX, own_copies, start)
    ret_r[me] = ret_s[me]
    each(NP, y_copies, wait)

    def add_up(q, _):
        sums = [jnp.zeros((QROWS, IDIM), jnp.float32) for _ in range(8)]
        for p in range(NP):
            block = want[p, 0, me * NZ + q]
            got = ret_r[p, q].astype(jnp.float32)
            for b in range(8):
                sums[b] = sums[b] + jnp.where(block == b, got, 0.0)
        for b in range(8):
            z_part[q, b] = sums[b].astype(jnp.bfloat16)
        return 0

    lax.fori_loop(0, NZ, add_up, 0)

    def z_copies(q):
        peer = ((z + place_offset(q)) % NZ) * NP + me
        return [remote(z_part.at[q], z_got.at[q], z_send.at[q], z_recv.at[q], (peer, h))]

    each(NZ, z_copies, start)
    each(NZ, z_copies, wait)
    cache_sum = z_part[0].astype(jnp.float32)
    for q in range(1, NZ):
        cache_sum = cache_sum + z_got[q].astype(jnp.float32)
    cache_g[:, h] = cache_sum

    def cache_copies(i):
        peer = (h + i) % NX
        return [
            remote(cache_g.at[:, h], cache_g.at[:, h], f_send.at[1, i], f_recv.at[1, i], (seq, peer))
        ]

    each(NX, cache_copies, start)
    each(NX, lg_copies, wait_send)
    out_div[...] = div[...]
    each(NX, own_copies, wait)
    own_store = pltpu.make_async_copy(own_g, out_own, out_sem.at[0])
    own_store.start()
    each(NX, cache_copies, wait)
    cache_store = pltpu.make_async_copy(cache_g, out_cache, out_sem.at[1])
    cache_store.start()
    own_store.wait()
    cache_store.wait()


def backward(mass, logits, query_index, index_gains, key_i, want):
    rows, iheads, _ = query_index.shape
    f32, bf16, sem = jnp.float32, jnp.bfloat16, pltpu.SemaphoreType.DMA
    vmem = pl.BlockSpec(memory_space=pltpu.VMEM)
    any_space = pl.BlockSpec(memory_space=pl.ANY)
    return pl.pallas_call(
        backward_kernel,
        out_shape=(
            jax.ShapeDtypeStruct((QBLK, 8, 128), f32),
            jax.ShapeDtypeStruct((rows, iheads, IDIM), bf16),
            jax.ShapeDtypeStruct((iheads, rows), f32),
            jax.ShapeDtypeStruct((8, NX, QROWS, IDIM), f32),
            jax.ShapeDtypeStruct((QBLK, NX, QROWS, IDIM), f32),
        ),
        in_specs=[vmem] * 5 + [pl.BlockSpec(memory_space=pltpu.SMEM)],
        out_specs=(vmem, vmem, vmem, any_space, any_space),
        scratch_shapes=[
            pltpu.VMEM((QBLK, BLK, SPAN), bf16),
            pltpu.VMEM((NX, BLK, SPAN), bf16),
            pltpu.VMEM((NX, BLK, SPAN), f32),
            pltpu.VMEM((QBLK, BLK, SPAN), bf16),
            pltpu.VMEM((QBLK, 8, 128), f32),
            pltpu.VMEM((SPAN, IDIM), f32),
            pltpu.VMEM((QBLK, 8, QROWS, IDIM), f32),
            pltpu.VMEM((QBLK, 8, NX, QROWS, IDIM), bf16),
            pltpu.VMEM((NX, QBLK, 8, QROWS, IDIM), bf16),
            pltpu.VMEM((QBLK * 8, QROWS, IDIM), bf16),
            pltpu.VMEM((NP, NZ, QROWS, IDIM), bf16),
            pltpu.VMEM((NP, NZ, QROWS, IDIM), bf16),
            pltpu.VMEM((NZ, 8, QROWS, IDIM), bf16),
            pltpu.VMEM((NZ, 8, QROWS, IDIM), bf16),
            pltpu.VMEM((8, NX, QROWS, IDIM), f32),
            pltpu.VMEM((QBLK, NX, QROWS, IDIM), f32),
            sem((2,)),
            sem((2, NX)),
            sem((2, NX)),
            sem((2, NX)),
            sem((2, NX)),
            sem((NX, QBLK)),
            sem((NX, QBLK)),
            sem((NP,)),
            sem((NP,)),
            sem((NZ,)),
            sem((NZ,)),
            sem((2, NX)),
            sem((2, NX)),
            pltpu.VMEM((2, iheads, 128), f32),
        ],
        compiler_params=pltpu.CompilerParams(
            collective_id=1, has_side_effects=True, vmem_limit_bytes=48 << 20
        ),
        name="backward",
    )(mass, logits, query_index, index_gains, key_i, want)


def per_device(
    query_latent,
    stretch_latent,
    cache_latent,
    query_index,
    stretch_index,
    cache_index,
    index_gains,
    block_ids,
):
    rows = query_latent.shape[0]
    key_l, key_i, want = gather_keys(
        block_ids, cache_latent, cache_index, stretch_latent, stretch_index
    )
    mass, logits = forward(query_latent, key_l, key_i, query_index, index_gains)
    divergence, qgrad, ggrad, cache_grad, own_grad = backward(
        mass.reshape(QBLK, BLK, SPAN),
        logits.reshape(QBLK, BLK, SPAN),
        query_index,
        index_gains.T,
        key_i,
        want,
    )
    return (
        divergence[:, 0, :BLK].reshape(rows),
        qgrad,
        ggrad.T,
        cache_grad.reshape(cache_index.shape),
        own_grad.reshape(stretch_index.shape),
    )


def solution(mesh):
    placed = (
        P("seq", "head", None),
        P("seq", None),
        P("seq", None),
        P("seq", "head", None),
        P("seq", None),
        P("seq", None),
        P("seq", "head"),
        P("seq", None),
    )
    return jax.shard_map(
        per_device,
        mesh=mesh,
        in_specs=placed,
        out_specs=(
            P("seq"),
            P("seq", "head", None),
            P("seq", "head"),
            P("seq", None),
            P("seq", None),
        ),
        check_vma=False,
    )
```

time: 397 us -> 159 us (0.40); the launches traced: 390 us -> 158 us
  waiting for transfers between devices: 194 us -> 0 us
  Pallas kernels: 0 us -> 147 us
  matrix products: 45.6 us -> 0 us
  local copies, waits for them, and re-layouts: 52.3 us -> 10.6 us
  other arithmetic: 40.5 us -> 0 us
  starting transfers between devices: 23 us -> 0 us
  blocking collectives: 20.2 us -> 0 us
  between operations: 14.8 us -> 0.7 us
    pallas_call x0 -> x3, Pallas kernels: none -> 147 us  [the longest x1 63.8 us: gather_keys(): pl.pallas_call(gather_kernel, out_shape=(jax.ShapeDtypeStruct((QBLK, 8, N...]
    all_to_all x3 -> x0, waiting for transfers between devices: 107 us -> none  [the longest x1 80.3 us: per_device(): lax.all_to_all(served_latent, 'seq', split_axis=0, concat_axis=0, tiled=T...]
    psum x2 -> x0, waiting for transfers between devices: 87.1 us -> none  [the longest x1 48.3 us: per_device(): mass_sum, logits = lax.psum((mass_part, logit_portion), 'head')]
    dot_general x7 -> x0, matrix products: 45.6 us -> none  [the longest x1 15.1 us: per_device(): jnp.einsum('nwh,nwgh->nwg', logit_gradient, live_heads, precision=lax.Pre...]
    all_to_all x3 -> x0, starting transfers between devices: 22.7 us -> none  [the longest x1 10.5 us: per_device(): lax.all_to_all(outgoing.astype(jnp.bfloat16), 'seq', split_axis=0, concat...]
    div x2 -> x0, other arithmetic: 20.2 us -> none  [the longest x1 18.8 us: attention_mass(): attention = shifted / jnp.sum(shifted, axis=-1, keepdims=True)]
    all_to_all x1 -> x0, blocking collectives: 20.2 us -> none  [per_device(): lax.all_to_all(request.reshape(seq_count, capacity), 'seq', split_axis=0,...]
    unnamed x33 -> x18, local copies, waits for them, and re-layouts: 26.8 us -> 9.9 us
  transfers between devices with their start and end apart: 5 -> 0, of which waited for: 5 -> 0; matrix products, arithmetic and copies ran while one was open for 17% -> 0% of each run, Pallas kernels for 0% -> 0%
where the time goes in v1:
time: 159 us; the launch traced here: 158 us
  Pallas kernels  147 us (92%)
  local copies, waits for them, and re-layouts  10.6 us (7%)
    pallas_call x1, Pallas kernels, gather_keys(): pl.pallas_call(gather_kernel, out_shape=(jax.ShapeDtypeStruct((QBLK, 8, N...  63.8 us
    pallas_call x1, Pallas kernels, backward(): pl.pallas_call(backward_kernel, out_shape=(jax.ShapeDtypeStruct((QBLK, 8,...  51.3 us
    pallas_call x1, Pallas kernels, forward(): pl.pallas_call(forward_kernel, grid=(QBLK // 2, heads // QUAD), in_specs=...  31.9 us
    unnamed x18, local copies, waits for them, and re-layouts  9.9 us

profile of v1, /device:TPU:32, one launch (start us, length us, event | category | flops | bytes accessed | tf_op | source)
XLA Modules:
  0.0 158.3 jit_solution(17391115804580420180)
XLA Ops:
  0.6 0.0 copy-start.1
  0.6 1.2 copy.14
  1.9 1.4 copy.13
  3.3 0.0 copy-start.2
  3.3 0.9 copy-done.2
  4.2 0.0 copy-start.4
  4.2 0.8 copy-done.4
  5.0 0.0 copy-start.5
  5.0 0.7 copy-done.5
  5.7 63.8 %gather_keys.1 = (bf16[4,8,4,16,576]{4,3,2,1,0:T(8,128)(2,1)S(1)}, bf16[4,8,4,16,128]{4,3,2,1,0:T(8,128)(2,1)S(1)}, s32[8,8,128]{2,1,0:T(8,128)S(1)}) custom-call(s32[4,7]{1,0:T(4,128)S(1)} %copy-done.5, bf16[8,4,16,576]{3,2,1,0:T(8,128)(2,1)S(1)} %bitcast.11, bf16[8,4,16,128]{3,2,1,0:T(8,128)(2,1)S(1)} %bitcast.16, bf16[4,4,16,576]{3,2,1,0:T(8,128)(2,1)S(1)} %bitcast.12, ...), custom_call_target="tpu_custom_call" | custom-call | tf_op jit(solution)/shard_map/gather_keys/pallas_call | solution.py:259
  69.5 0.0 copy-start
  69.5 1.2 copy-done
  70.7 0.0 copy-start.3
  70.7 0.7 copy-done.3
  71.5 31.9 %forward.1 = (f32[256,512]{1,0:T(8,128)S(1)}, f32[256,512]{1,0:T(8,128)S(1)}) custom-call(bf16[32,576,256]{2,1,0:T(8,128)(2,1)} %bitcast.22, bf16[4,8,4,16,576]{4,3,2,1,0:T(8,128)(2,1)S(1)} %get-tuple-element.15.key_l, bf16[4,8,4,16,128]{4,3,2,1,0:T(8,128)(2,1)S(1)} %get-tuple-element.16.key_i, bf16[256,16,128]{2,1,0:T(8,128)(2,1)S(1)} %copy-done, ...), custom_call_target="tpu_custom_call" | custom-call | tf_op jit(solution)/shard_map/forward/pallas_call | solution.py:359
  103.4 0.0 copy-done.1
  103.4 51.3 %backward.1 = (f32[4,8,128]{2,1,0:T(8,128)S(1)}, bf16[256,16,128]{2,1,0:T(8,128)(2,1)S(1)}, f32[16,256]{1,0:T(8,128)S(1)}, f32[8,4,16,128]{3,2,1,0:T(8,128)S(1)}, f32[4,4,16,128]{3,2,1,0:T(8,128)S(1)}) custom-call(f32[4,64,512]{2,1,0:T(8,128)S(1)} %bitcast.13, f32[4,64,512]{2,1,0:T(8,128)S(1)} %bitcast.14, bf16[256,16,128]{2,1,0:T(8,128)(2,1)S(1)} %copy-done.1, ...), custom_call_target="tpu_custom_call" | custom-call | tf_op jit(solution)/shard_map/backward/pallas_call | solution.py:676
  154.7 0.6 reshape_squeeze.3
  155.3 1.0 copy.19
  156.3 0.6 copy.20
  156.9 0.7 copy.21
  157.6 0.7 copy.22
  (1 shorter events, 0.0 us)
Async XLA Ops:
  0.6 102.8 %copy-start.1 = (bf16[256,16,128]{2,1,0:T(8,128)(2,1)S(1)}, bf16[256,16,128]{2,1,0:T(8,128)(2,1)}, u32[]{:S(2)}) copy-start(bf16[256,16,128]{2,1,0:T(8,128)(2,1)} %qi.3) | copy-start | bytes 3145732
  3.3 0.9 copy-start.2
  4.2 0.8 copy-start.4
  5.0 0.7 copy-start.5
  69.5 1.2 copy-start
  70.7 0.7 copy-start.3

commit v2 on v0

v2 whole, which is shorter than its diff:
```python
import jax
import jax.numpy as jnp
from jax import lax
from jax.experimental import pallas as pl
from jax.experimental.pallas import tpu as pltpu
from jax.sharding import PartitionSpec as P

MESH = pl.DeviceIdType.MESH
HEADS = 128
SCORE_SCALE = 192.0 ** (-0.5)
LOG2E = 1.4426950408889634
BLK = 64
PICKED = 7
QBLK = 4
NX = 4
NZ = 8
NP = 8
QROWS = BLK // NX
KDIM = 576
IDIM = 128
SPAN = 512
HEAD_A = 256
WIDE_A, WIDE_B = IDIM + HEAD_A, KDIM - HEAD_A
OCT = 8
LOCAL_HEADS = 32
NOCT = LOCAL_HEADS // OCT
IHEADS = 16
PART = 16
ROWS = QBLK * BLK
CACHED = 512


def z_place(offset):
    return jnp.where(offset == 0, 0, jnp.where(offset <= 4, 2 * offset - 1, 2 * (8 - offset)))


def place_offset(place):
    return jnp.where(place % 2 == 1, (place + 1) // 2, NZ - place // 2)


def kernel(ids, cl, ci, sl, si, q, qi_h, gains_h, out_div, out_qgrad, out_ggrad, out_cache, out_own, *scratch):
    refs = list(scratch)
    take = lambda n: [refs.pop(0) for _ in range(n)]
    stock_a, stock_b = take(NZ), take(NZ)
    send_a, send_b, recv_a, recv_b, key_a, key_b, want_v, want_s = take(8)
    cl_v, sl_v, q_v, qr, qi, gains = take(6)
    sums, mass_o, mass_b, logits, rs_m, rs_l, lg, div = take(8)
    kgrad, kquarter, kpart, krecv, slots, ret_s, ret_r, z_part, z_got, cache_g, own_g = take(11)
    qgrad_v, ggrad_t = take(2)
    load_sem, q_sem, out_sem, ids_send, ids_recv, zs_send, zs_recv, ys_send, ys_recv = take(9)
    xs_send, xs_recv, rs_send, rs_recv, lg_send, lg_recv, k_send, k_recv = take(8)
    y_send, y_recv, z_send, z_recv, f_send, f_recv = take(6)

    seq = lax.axis_index("seq")
    h = lax.axis_index("head")
    z, me = seq // NP, seq % NP
    z_next, z_prev = ((z + 1) % NZ) * NP + me, ((z + NZ - 1) % NZ) * NP + me
    x_next, x_prev = (h + 1) % NX, (h + NX - 1) % NX
    quarter = pl.ds(pl.multiple_of(h * QROWS, QROWS), QROWS)

    def remote(src, dst, send, recv, target):
        return pltpu.make_async_remote_copy(
            src_ref=src,
            dst_ref=dst,
            send_sem=send,
            recv_sem=recv,
            device_id=target,
            device_id_type=MESH,
        )

    def each(count, copies, act):
        def body(i, _):
            for copy in copies(i):
                act(copy)
            return 0

        lax.fori_loop(1, count, body, 0)

    start = lambda copy: copy.start()
    wait = lambda copy: copy.wait()
    wait_recv = lambda copy: copy.wait_recv()
    wait_send = lambda copy: copy.wait_send()

    load_cl = pltpu.make_async_copy(cl, cl_v, load_sem.at[0])
    load_ci = pltpu.make_async_copy(ci.at[:, h], stock_a[0].at[:, :, pl.ds(0, IDIM)], load_sem.at[1])
    load_sl = pltpu.make_async_copy(sl, sl_v, load_sem.at[2])
    load_si = pltpu.make_async_copy(
        si, key_a.at[:, PICKED, :, :, pl.ds(0, IDIM)], load_sem.at[3]
    )
    load_qi = pltpu.make_async_copy(qi_h, qi, load_sem.at[4])
    load_gains = pltpu.make_async_copy(gains_h, gains, load_sem.at[5])
    load_q = [
        pltpu.make_async_copy(
            q.at[pl.ds(o * OCT, OCT)], q_v.at[pl.ds(o * OCT, OCT)], q_sem.at[o]
        )
        for o in range(NOCT)
    ]
    for load in [load_cl, load_ci, load_sl, load_si, *load_q, load_qi, load_gains]:
        load.start()

    barrier = pltpu.get_barrier_semaphore()

    def greet(count, target):
        def body(i, _):
            pl.semaphore_signal(barrier, inc=1, device_id=target(i), device_id_type=MESH)
            return 0

        lax.fori_loop(1, count, body, 0)

    greet(NZ, lambda i: (((z + i) % NZ) * NP + me, h))
    greet(NP, lambda i: (z * NP + (me + i) % NP, h))
    greet(NX, lambda i: (seq, (h + i) % NX))

    lane = lax.broadcasted_iota(jnp.int32, (8, 128), 1)
    row = lax.broadcasted_iota(jnp.int32, (8, 128), 0)
    tile = jnp.full((8, 128), -1, jnp.int32)
    for r in range(QBLK):
        for j in range(PICKED):
            block = ids[r, j]
            owner = block >> 3
            spot = (owner & 7) * NZ + z_place(((owner >> 3) - z + NZ) & 7)
            value = jnp.where(row == 0, block & 7, r * 8 + j)
            tile = jnp.where(lane == spot, value, tile)
    want_v[me] = tile

    load_cl.wait()
    for b in range(8):
        if b % 2 == 0:
            pair = cl_v[:, b * BLK : (b + 2) * BLK].T
        rows = pair[(b % 2) * BLK : (b % 2 + 1) * BLK].reshape(NX, QROWS, KDIM)
        mine = jnp.where(
            h == 0, rows[0], jnp.where(h == 1, rows[1], jnp.where(h == 2, rows[2], rows[3]))
        )
        stock_a[0][b, :, IDIM:] = mine[:, :HEAD_A]
        stock_b[0][b] = mine[:, HEAD_A:]
    load_ci.wait()
    pl.semaphore_wait(barrier, NX - 1 + NP - 1 + NZ - 1)

    def ids_copies(i):
        peer = (me + i) % NP
        return [
            remote(want_v.at[me], want_v.at[me], ids_send.at[i], ids_recv.at[i], (z * NP + peer, h))
        ]

    def zs_copy(a, step, way):
        stock = stock_b if a else stock_a
        if way == 0:
            src, dst = 2 * (step - 1), 2 * step if step < 4 else 7
            part, target = pl.ds(0, 4), z_next
        else:
            src, dst = max(2 * step - 3, 0), 2 * step - 1
            part, target = pl.ds(4, 4), z_prev
        if step < 4:
            part = pl.ds(0, 8)
        return remote(
            stock[src].at[part],
            stock[dst].at[part],
            zs_send.at[a, way, step],
            zs_recv.at[a, way, step],
            (target, h),
        )

    spans = ((0, 1), (1, 2), (3, 2), (5, 2), (7, 1))

    def ys_copy(a, step, i):
        first, count = spans[step]
        peer = (me + i) % NP
        send, recv = (send_b, recv_b) if a else (send_a, recv_a)
        return remote(
            send.at[peer, pl.ds(first, count)],
            recv.at[me, pl.ds(first, count)],
            ys_send.at[a, step, i],
            ys_recv.at[a, step, i],
            (z * NP + peer, h),
        )

    def stage(a, step):
        first, count = spans[step]
        stock, send, recv = (stock_b, send_b, recv_b) if a else (stock_a, send_a, recv_a)

        def body(i, _):
            peer = (me + i) % NP
            for p in range(first, first + count):
                block = jnp.maximum(want_s[peer, 0, me * NZ + p], 0)
                send[peer, p] = stock[p][block]
            ys_copy(a, step, i).start()
            return 0

        lax.fori_loop(1, NP, body, 0)
        for p in range(first, first + count):
            block = jnp.maximum(want_s[me, 0, me * NZ + p], 0)
            recv[me, p] = stock[p][block]

    def turn(a, step):
        for way in range(2):
            zs_copy(a, step, way).wait_recv()
            if step < 4:
                zs_copy(a, step + 1, way).start()

    def arrange(unit):
        p, o = unit % 2, unit // 2
        if p == 0:
            load_q[o].wait()
        for half in range(2):
            cut = slice(p * 128 + half * BLK, p * 128 + (half + 1) * BLK)
            qr[p * 2 + half, o] = jnp.concatenate(
                [q_v[o * OCT + i, :, cut] for i in range(OCT)], axis=1
            )

    for way in range(2):
        zs_copy(0, 1, way).start()
    for way in range(2):
        zs_copy(1, 1, way).start()
    each(NP, ids_copies, start)
    each(NP, ids_copies, wait)
    to_scalar = pltpu.make_async_copy(want_v, want_s, load_sem.at[6])
    to_scalar.start()
    to_scalar.wait()
    stage(0, 0)
    stage(1, 0)
    arrange(0)
    for step in range(1, 5):
        turn(0, step)
        stage(0, step)
        arrange(2 * step - 1)
        turn(1, step)
        stage(1, step)
        if step < 4:
            arrange(2 * step)

    load_sl.wait()
    for p in range(2):
        rows = sl_v[:, p * 128 : (p + 1) * 128].T
        for half in range(2):
            own = rows[half * BLK : (half + 1) * BLK].reshape(NX, QROWS, KDIM)
            key_a[2 * p + half, PICKED, :, :, IDIM:] = own[:, :, :HEAD_A]
            key_b[2 * p + half, PICKED] = own[:, :, HEAD_A:]
    load_si.wait()

    def gathered(a):
        for step in range(len(spans)):
            each(NP, lambda i: [ys_copy(a, step, i)], wait)
        key, recv = (key_b, recv_b) if a else (key_a, recv_a)
        for r in range(QBLK):
            for j in range(PICKED):
                owner = ids[r, j] >> 3
                place = z_place(((owner >> 3) - z + NZ) & 7)
                key[r, j, h] = recv[owner & 7, place]

    def xs_copy(a, r, step, way):
        if step == 0:
            rows, part = h, pl.ds(0, PICKED)
        elif way == 0:
            rows, part = x_prev, pl.ds(0, 4)
        else:
            rows, part = x_next, pl.ds(4, 3)
        spot = (key_b if a else key_a).at[r, part, rows]
        return remote(
            spot,
            spot,
            xs_send.at[a, r, step, way],
            xs_recv.at[a, r, step, way],
            (seq, x_prev if way else x_next),
        )

    def xs_start(a, r):
        for way in range(2):
            xs_copy(a, r, 0, way).start()

    def xs_turn(a, r):
        for way in range(2):
            xs_copy(a, r, 0, way).wait_recv()
        for way in range(2):
            xs_copy(a, r, 1, way).start()

    def xs_done(a, r):
        for way in range(2):
            xs_copy(a, r, 1, way).wait_recv()

    gathered(0)
    for r in range(QBLK):
        xs_start(0, r)
    gathered(1)
    for r in range(QBLK):
        xs_turn(0, r)
        xs_start(1, r)

    def rs_copies(a, r):
        src, dst = (mass_b, rs_m) if a else (logits, rs_l)
        return remote(src.at[r], dst.at[h], rs_send.at[a, r], rs_recv.at[a, h], (seq, r))

    def rs_start(a, r):
        @pl.when(h != r)
        def _():
            rs_copies(a, r).start()

    def ikeys_of(r):
        return key_a[r, :, :, :, :IDIM].reshape(SPAN, IDIM)

    def gain_of(r, first):
        half = gains[:, (r // 2) * 128 : (r // 2 + 1) * 128]
        return pltpu.roll(half, 128 - (r % 2) * BLK - first, 1)

    def make_logits(r):
        ikeys = ikeys_of(r)

        def body(c, _):
            first = pl.multiple_of(c * PART, PART)
            iblock = qi[pl.ds(r * BLK + first, PART)].reshape(PART * IHEADS, IDIM)
            inner = lax.dot_general(
                iblock, ikeys, (((1,), (1,)), ((), ())), preferred_element_type=jnp.float32
            )
            gain = gain_of(r, first)
            rows = []
            for t in range(PART):
                live = jnp.maximum(inner[t * IHEADS : (t + 1) * IHEADS], 0.0)
                rows.append(jnp.sum(live * gain[:, t : t + 1], axis=0, keepdims=True))
            logits[r, pl.ds(first, PART)] = jnp.concatenate(rows, axis=0)
            return 0

        lax.fori_loop(0, BLK // PART, body, 0)
        rs_start(0, r)

    def make_mass(r):
        keys = jnp.concatenate(
            [
                key_a[r, :, :, :, IDIM:].reshape(SPAN, HEAD_A),
                key_b[r].reshape(SPAN, WIDE_B),
            ],
            axis=1,
        )
        cut = PICKED * BLK
        scale = SCORE_SCALE * LOG2E
        own_row = lax.broadcasted_iota(jnp.int32, (BLK, OCT * BLK), 0)
        token = lax.broadcasted_iota(jnp.int32, (BLK, OCT * BLK), 1) % BLK
        allowed = own_row <= token
        sums[...] = jnp.zeros_like(sums)

        def body(o, _):
            scores = jnp.dot(keys, qr[r, o], preferred_element_type=jnp.float32)
            old, own = scores[:cut], jnp.where(allowed, scores[cut:], -jnp.inf)
            top = jnp.maximum(
                jnp.max(old, axis=0, keepdims=True), jnp.max(own, axis=0, keepdims=True)
            )
            e_old = jnp.exp2((old - top) * scale)
            e_own = jnp.exp2((own - top) * scale)
            total = jnp.sum(e_old, axis=0, keepdims=True) + jnp.sum(e_own, axis=0, keepdims=True)
            share = 1.0 / total
            for lo, hi, e in ((0, cut, e_old), (cut, SPAN, e_own)):
                part = e * share
                fold = part[:, :128]
                for i in range(1, OCT // 2):
                    fold = fold + part[:, i * 128 : (i + 1) * 128]
                sums[lo:hi] += fold
            return 0

        lax.fori_loop(0, NOCT, body, 0)
        mass = (sums[:, :BLK] + sums[:, BLK:]).T

        @pl.when(h == r)
        def _():
            mass_o[...] = mass

        mass_b[r] = mass.astype(jnp.bfloat16)
        rs_start(1, r)

    def lg_copies(r, i):
        peer = (h + i) % NX
        return [
            remote(lg.at[r], lg.at[r], lg_send.at[0, i], lg_recv.at[0, r], (seq, peer)),
            remote(div.at[r], div.at[r], lg_send.at[1, i], lg_recv.at[1, r], (seq, peer)),
        ]

    def divergence_of(r):
        for i in range(1, NX):
            peer = (h + i) % NX
            for a, (src, dst) in enumerate(((logits, rs_l), (mass_b, rs_m))):
                remote(
                    src.at[r], dst.at[peer], rs_send.at[a, r], rs_recv.at[a, peer], (seq, peer)
                ).wait_recv()
        mass_sum, logit = mass_o[...], logits[r]
        for i in range(1, NX):
            mass_sum = mass_sum + rs_m[(h + i) % NX].astype(jnp.float32)
            logit = logit + rs_l[(h + i) % NX]
        target = mass_sum * (1.0 / HEADS)
        column = lax.broadcasted_iota(jnp.int32, (BLK, SPAN), 1)
        token = lax.broadcasted_iota(jnp.int32, (BLK, SPAN), 0)
        allowed = column - PICKED * BLK <= token
        masked = jnp.where(allowed, logit, -jnp.inf)
        shifted = masked - jnp.max(masked, axis=1, keepdims=True)
        powers = jnp.exp(shifted)
        total = jnp.sum(powers, axis=1, keepdims=True)
        model = powers / total
        log_model = jnp.where(allowed, shifted - jnp.log(total), 0.0)
        safe = jnp.where(target > 0, target, 1.0)
        pointwise = jnp.where(allowed, target * (jnp.log(safe) - log_model), 0.0)
        divergence = jnp.sum(pointwise, axis=1, keepdims=True)
        lg[r] = jnp.where(allowed, model - target, 0.0).astype(jnp.bfloat16)
        each(NX, lambda i: lg_copies(r, i)[:1], start)
        diagonal = lax.broadcasted_iota(jnp.int32, (BLK, 128), 0) == lax.broadcasted_iota(
            jnp.int32, (BLK, 128), 1
        )
        in_lanes = jnp.sum(jnp.where(diagonal, divergence, 0.0), axis=0, keepdims=True)
        div[r] = jnp.broadcast_to(in_lanes, (8, 128))
        each(NX, lambda i: lg_copies(r, i)[1:], start)

    def k_copy(i, r):
        peer = (h + i) % NX
        return remote(
            kpart.at[r, :, peer], krecv.at[h, r], k_send.at[i, r], k_recv.at[i, r], (seq, peer)
        )

    def qgrad_copy(r):
        rows = pl.ds(r * BLK, BLK)
        return pltpu.make_async_copy(qgrad_v.at[rows], out_qgrad.at[rows], out_sem.at[r])

    def backward(r):
        @pl.when(h != r)
        def _():
            lg_copies(r, 1)[0].wait_recv()

        ikeys = ikeys_of(r)
        kgrad[...] = jnp.zeros_like(kgrad)
        ggrad_t[...] = jnp.zeros_like(ggrad_t)

        def body(c, _):
            first = pl.multiple_of(c * PART, PART)
            rows = pl.ds(r * BLK + first, PART)
            iblock = qi[rows].reshape(PART * IHEADS, IDIM)
            inner = lax.dot_general(
                iblock, ikeys, (((1,), (1,)), ((), ())), preferred_element_type=jnp.float32
            )
            slope = lg[r, pl.ds(first, PART)].astype(jnp.float32)
            gain = gain_of(r, first)
            lanes = lax.broadcasted_iota(jnp.int32, (IHEADS, 128), 1)
            found = jnp.zeros((IHEADS, 128), jnp.float32)
            grads = []
            for t in range(PART):
                piece = inner[t * IHEADS : (t + 1) * IHEADS]
                push = slope[t : t + 1]
                gsum = jnp.sum(jnp.maximum(piece, 0.0) * push, axis=1, keepdims=True)
                found = jnp.where(lanes == first + t, gsum, found)
                grads.append(
                    jnp.where(piece > 0, push * gain[:, t : t + 1], 0.0).astype(jnp.bfloat16)
                )
            ggrad_t[...] += found
            inner_grad = jnp.concatenate(grads, axis=0)
            qgrad = jnp.dot(inner_grad, ikeys, preferred_element_type=jnp.float32)
            qgrad_v[rows] = qgrad.astype(jnp.bfloat16).reshape(PART, IHEADS, IDIM)
            kgrad[...] += lax.dot_general(
                inner_grad, iblock, (((0,), (0,)), ((), ())), preferred_element_type=jnp.float32
            )
            return 0

        lax.fori_loop(0, BLK // PART, body, 0)
        for j in range(8):
            block = kgrad[pl.ds(j * BLK, BLK)].reshape(NX, QROWS, IDIM)
            kpart[r, j] = block.astype(jnp.bfloat16)
            kquarter[r, j] = kgrad[pl.ds(pl.multiple_of(j * BLK + h * QROWS, QROWS), QROWS)]
        each(NX, lambda i: [k_copy(i, r)], start)
        qgrad_copy(r).start()
        out_ggrad[:, r * BLK : (r + 1) * BLK] = ggrad_t[:, :BLK]

    def owner_step(r):
        @pl.when(h == r)
        def _():
            divergence_of(r)

    load_qi.wait()
    load_gains.wait()
    for r in range(QBLK):
        xs_done(0, r)
        make_logits(r)
        if r < QBLK - 1:
            xs_turn(1, r)
    for r in range(QBLK):
        xs_done(1, r)
        make_mass(r)
        if r == 0:
            xs_turn(1, QBLK - 1)
        if r >= 1:
            owner_step(r - 1)
        if r >= 2:
            backward(r - 2)
    owner_step(QBLK - 1)
    backward(QBLK - 2)
    backward(QBLK - 1)

    for r in range(QBLK):
        each(NX, lambda i: [k_copy(i, r)], wait)
        total = kquarter[r]
        for i in range(1, NX):
            total = total + krecv[(h + i) % NX, r].astype(jnp.float32)
        own_g[r, h] = total[PICKED]
        slots[pl.ds(r * 8, 8)] = total.astype(jnp.bfloat16)

    def put_back(p, _):
        for place in range(NZ):
            slot = jnp.maximum(want_s[me, 1, p * NZ + place], 0)
            ret_s[p, place] = slots[slot]
        return 0

    lax.fori_loop(0, NP, put_back, 0)

    def y_copies(i):
        peer = (me + i) % NP
        return [
            remote(ret_s.at[peer], ret_r.at[me], y_send.at[i], y_recv.at[i], (z * NP + peer, h))
        ]

    each(NP, y_copies, start)

    def own_copies(i):
        peer = (h + i) % NX
        return [remote(own_g.at[:, h], own_g.at[:, h], f_send.at[0, i], f_recv.at[0, i], (seq, peer))]

    each(NX, own_copies, start)
    ret_r[me] = ret_s[me]
    each(NP, y_copies, wait)

    def z_copies(place):
        peer = ((z + place_offset(place)) % NZ) * NP + me
        return [remote(z_part.at[place], z_got.at[place], z_send.at[place], z_recv.at[place], (peer, h))]

    def add_up(place, _):
        sums8 = [jnp.zeros((QROWS, IDIM), jnp.float32) for _ in range(8)]
        for p in range(NP):
            block = want_s[p, 0, me * NZ + place]
            got = ret_r[p, place].astype(jnp.float32)
            for b in range(8):
                sums8[b] = sums8[b] + jnp.where(block == b, got, 0.0)
        for b in range(8):
            z_part[place, b] = sums8[b].astype(jnp.bfloat16)

        @pl.when(place > 0)
        def _():
            for copy in z_copies(place):
                copy.start()

        return 0

    lax.fori_loop(0, NZ, add_up, 0)

    for step in range(1, 5):
        for way in range(2):
            for a in range(2):
                zs_copy(a, step, way).wait_send()
    for a in range(2):
        for r in range(QBLK):
            for step in range(2):
                for way in range(2):
                    xs_copy(a, r, step, way).wait_send()
    for r in range(QBLK):

        @pl.when(h != r)
        def _():
            rs_copies(0, r).wait_send()
            rs_copies(1, r).wait_send()
            lg_copies(r, 1)[1].wait_recv()

        @pl.when(h == r)
        def _():
            each(NX, lambda i: lg_copies(r, i), wait_send)

    out_div[...] = div[...]
    for r in range(QBLK):
        qgrad_copy(r).wait()

    each(NZ, z_copies, wait)
    cache_sum = z_part[0].astype(jnp.float32)
    for place in range(1, NZ):
        cache_sum = cache_sum + z_got[place].astype(jnp.float32)
    cache_g[:, h] = cache_sum

    def cache_copies(i):
        peer = (h + i) % NX
        return [
            remote(cache_g.at[:, h], cache_g.at[:, h], f_send.at[1, i], f_recv.at[1, i], (seq, peer))
        ]

    each(NX, cache_copies, start)
    each(NX, own_copies, wait)
    own_store = pltpu.make_async_copy(own_g, out_own, out_sem.at[4])
    own_store.start()
    each(NX, cache_copies, wait)
    cache_store = pltpu.make_async_copy(cache_g, out_cache, out_sem.at[5])
    cache_store.start()
    own_store.wait()
    cache_store.wait()


def per_device(
    query_latent,
    stretch_latent,
    cache_latent,
    query_index,
    stretch_index,
    cache_index,
    index_gains,
    block_ids,
):
    f32, bf16, sem, V = jnp.float32, jnp.bfloat16, pltpu.SemaphoreType.DMA, pltpu.VMEM
    vmem = pl.BlockSpec(memory_space=pltpu.VMEM)
    any_space = pl.BlockSpec(memory_space=pl.ANY)
    divergence, qgrad, ggrad, cache_grad, own_grad = pl.pallas_call(
        kernel,
        out_shape=(
            jax.ShapeDtypeStruct((QBLK, 8, 128), f32),
            jax.ShapeDtypeStruct((ROWS, IHEADS, IDIM), bf16),
            jax.ShapeDtypeStruct((IHEADS, ROWS), f32),
            jax.ShapeDtypeStruct((8, NX, QROWS, IDIM), f32),
            jax.ShapeDtypeStruct((QBLK, NX, QROWS, IDIM), f32),
        ),
        in_specs=[pl.BlockSpec(memory_space=pltpu.SMEM)] + [any_space] * 7,
        out_specs=(vmem, any_space, vmem, any_space, any_space),
        scratch_shapes=[
            *[V((8, QROWS, WIDE_A), bf16)] * NZ,
            *[V((8, QROWS, WIDE_B), bf16)] * NZ,
            V((NP, NZ, QROWS, WIDE_A), bf16),
            V((NP, NZ, QROWS, WIDE_B), bf16),
            V((NP, NZ, QROWS, WIDE_A), bf16),
            V((NP, NZ, QROWS, WIDE_B), bf16),
            V((QBLK, 8, NX, QROWS, WIDE_A), bf16),
            V((QBLK, 8, NX, QROWS, WIDE_B), bf16),
            V((NP, 8, 128), jnp.int32),
            pltpu.SMEM((NP, 8, 128), jnp.int32),
            V((KDIM, CACHED), bf16),
            V((KDIM, ROWS), bf16),
            V((LOCAL_HEADS, KDIM, ROWS), bf16),
            V((QBLK, NOCT, KDIM, OCT * BLK), bf16),
            V((ROWS, IHEADS, IDIM), bf16),
            V((IHEADS, ROWS), f32),
            V((SPAN, 128), f32),
            V((BLK, SPAN), f32),
            V((QBLK, BLK, SPAN), bf16),
            V((QBLK, BLK, SPAN), f32),
            V((NX, BLK, SPAN), bf16),
            V((NX, BLK, SPAN), f32),
            V((QBLK, BLK, SPAN), bf16),
            V((QBLK, 8, 128), f32),
            V((SPAN, IDIM), f32),
            V((QBLK, 8, QROWS, IDIM), f32),
            V((QBLK, 8, NX, QROWS, IDIM), bf16),
            V((NX, QBLK, 8, QROWS, IDIM), bf16),
            V((QBLK * 8, QROWS, IDIM), bf16),
            V((NP, NZ, QROWS, IDIM), bf16),
            V((NP, NZ, QROWS, IDIM), bf16),
            V((NZ, 8, QROWS, IDIM), bf16),
            V((NZ, 8, QROWS, IDIM), bf16),
            V((8, NX, QROWS, IDIM), f32),
            V((QBLK, NX, QROWS, IDIM), f32),
            V((ROWS, IHEADS, IDIM), bf16),
            V((IHEADS, 128), f32),
            sem((7,)),
            sem((NOCT,)),
            sem((6,)),
            sem((NP,)),
            sem((NP,)),
            sem((2, 2, 5)),
            sem((2, 2, 5)),
            sem((2, 5, NP)),
            sem((2, 5, NP)),
            sem((2, QBLK, 2, 2)),
            sem((2, QBLK, 2, 2)),
            sem((2, QBLK)),
            sem((2, NX)),
            sem((2, NX)),
            sem((2, QBLK)),
            sem((NX, QBLK)),
            sem((NX, QBLK)),
            sem((NP,)),
            sem((NP,)),
            sem((NZ,)),
            sem((NZ,)),
            sem((2, NX)),
            sem((2, NX)),
        ],
        compiler_params=pltpu.CompilerParams(
            collective_id=0, has_side_effects=True, vmem_limit_bytes=60 << 20
        ),
        name="indexer_kl",
    )(
        block_ids,
        cache_latent.T,
        cache_index.reshape(8, NX, QROWS, IDIM),
        stretch_latent.T,
        stretch_index.reshape(QBLK, NX, QROWS, IDIM),
        jnp.transpose(query_latent, (1, 2, 0)),
        query_index,
        index_gains.T,
    )
    return (
        divergence[:, 0, :BLK].reshape(ROWS),
        qgrad,
        ggrad.T,
        cache_grad.reshape(CACHED, IDIM),
        own_grad.reshape(ROWS, IDIM),
    )


def solution(mesh):
    placed = (
        P("seq", "head", None),
        P("seq", None),
        P("seq", None),
        P("seq", "head", None),
        P("seq", None),
        P("seq", None),
        P("seq", "head"),
        P("seq", None),
    )
    return jax.shard_map(
        per_device,
        mesh=mesh,
        in_specs=placed,
        out_specs=(
            P("seq"),
            P("seq", "head", None),
            P("seq", "head"),
            P("seq", None),
            P("seq", None),
        ),
        check_vma=False,
    )
```

time: 397 us -> 130 us (0.33); the launches traced: 390 us -> 129 us
  waiting for transfers between devices: 194 us -> 0 us
  Pallas kernels: 0 us -> 121 us
  matrix products: 45.6 us -> 0 us
  local copies, waits for them, and re-layouts: 52.3 us -> 8.31 us
  other arithmetic: 40.5 us -> 0 us
  starting transfers between devices: 23 us -> 0 us
  blocking collectives: 20.2 us -> 0 us
  between operations: 14.8 us -> 0.64 us
    pallas_call x0 -> x1, Pallas kernels: none -> 121 us  [per_device(): pl.pallas_call(kernel, out_shape=(jax.ShapeDtypeStruct((QBLK, 8, 128), f3...]
    all_to_all x3 -> x0, waiting for transfers between devices: 107 us -> none  [the longest x1 80.3 us: per_device(): lax.all_to_all(served_latent, 'seq', split_axis=0, concat_axis=0, tiled=T...]
    psum x2 -> x0, waiting for transfers between devices: 87.1 us -> none  [the longest x1 48.3 us: per_device(): mass_sum, logits = lax.psum((mass_part, logit_portion), 'head')]
    dot_general x7 -> x0, matrix products: 45.6 us -> none  [the longest x1 15.1 us: per_device(): jnp.einsum('nwh,nwgh->nwg', logit_gradient, live_heads, precision=lax.Pre...]
    all_to_all x3 -> x0, starting transfers between devices: 22.7 us -> none  [the longest x1 10.5 us: per_device(): lax.all_to_all(outgoing.astype(jnp.bfloat16), 'seq', split_axis=0, concat...]
    div x2 -> x0, other arithmetic: 20.2 us -> none  [the longest x1 18.8 us: attention_mass(): attention = shifted / jnp.sum(shifted, axis=-1, keepdims=True)]
    all_to_all x1 -> x0, blocking collectives: 20.2 us -> none  [per_device(): lax.all_to_all(request.reshape(seq_count, capacity), 'seq', split_axis=0,...]
    unnamed x33 -> x4, local copies, waits for them, and re-layouts: 26.8 us -> 6.93 us
  transfers between devices with their start and end apart: 5 -> 0, of which waited for: 5 -> 0; matrix products, arithmetic and copies ran while one was open for 17% -> 0% of each run, Pallas kernels for 0% -> 0%
where the time goes in v2:
time: 130 us; the launch traced here: 129 us
  Pallas kernels  121 us (93%)
  local copies, waits for them, and re-layouts  8.31 us (6%)
    pallas_call x1, Pallas kernels, per_device(): pl.pallas_call(kernel, out_shape=(jax.ShapeDtypeStruct((QBLK, 8, 128), f3...  121 us
    unnamed x4, local copies, waits for them, and re-layouts  6.93 us

profile of v2, /device:TPU:32, one launch (start us, length us, event | category | flops | bytes accessed | tf_op | source)
XLA Modules:
  0.0 129.5 jit_solution(9282648184089261239)
XLA Ops:
  0.6 120.5 %indexer_kl.1 = (f32[4,8,128]{2,1,0:T(8,128)}, bf16[256,16,128]{2,1,0:T(8,128)(2,1)}, f32[16,256]{1,0:T(8,128)}, f32[8,4,16,128]{3,2,1,0:T(8,128)}, f32[4,4,16,128]{3,2,1,0:T(8,128)}) custom-call(s32[4,7]{1,0:T(4,128)} %ids.1, bf16[576,512]{1,0:T(8,128)(2,1)} %bitcast.10, bf16[8,4,16,128]{3,2,1,0:T(8,128)(2,1)} %bitcast.13, bf16[576,256]{1,0:T(8,128)(2,1)} %bitcast.11, ...), custom_call_target="tpu_custom_call" | custom-call | tf_op jit(solution)/shard_map/indexer_kl/pallas_call | solution.py:605
  121.1 0.7 slice_reduce_fusion
  121.9 0.6 reshape_squeeze.3
  122.5 2.4 %copy.17 = bf16[256,16,128]{2,1,0:T(8,128)(2,1)} copy(bf16[256,16,128]{2,1,0:T(8,128)(2,1)} %get-tuple-element.21) | data formatting | bytes 2097152
  124.9 1.3 %copy.18 = f32[256,16]{0,1:T(8,128)} copy(f32[256,16]{0,1:T(8,128)} %bitcast.17) | data formatting | bytes 32768
  126.2 1.7 %copy.19 = f32[512,128]{1,0:T(8,128)} copy(f32[512,128]{1,0:T(8,128)} %bitcast.12) | data formatting | bytes 524288
  127.9 1.6 %copy.20 = f32[256,128]{1,0:T(8,128)} copy(f32[256,128]{1,0:T(8,128)} %bitcast.14) | data formatting | bytes 262144

commit v3 on v2

--- a/solution.py
+++ b/solution.py
@@ -10,6 +10,7 @@
 SCORE_SCALE = 192.0 ** (-0.5)
 LOG2E = 1.4426950408889634
 BLK = 64
+LAG = 2
 PICKED = 7
 QBLK = 4
 NX = 4
@@ -46,7 +47,7 @@
     cl_v, sl_v, q_v, qr, qi, gains = take(6)
     sums, mass_o, mass_b, logits, rs_m, rs_l, lg, div = take(8)
     kgrad, kquarter, kpart, krecv, slots, ret_s, ret_r, z_part, z_got, cache_g, own_g = take(11)
-    qgrad_v, ggrad_t = take(2)
+    ggrad_t, qgrad_v, ggrad_v, div_v = take(4)
     load_sem, q_sem, out_sem, ids_send, ids_recv, zs_send, zs_recv, ys_send, ys_recv = take(9)
     xs_send, xs_recv, rs_send, rs_recv, lg_send, lg_recv, k_send, k_recv = take(8)
     y_send, y_recv, z_send, z_recv, f_send, f_recv = take(6)
@@ -207,36 +208,6 @@
                 [q_v[o * OCT + i, :, cut] for i in range(OCT)], axis=1
             )
 
-    for way in range(2):
-        zs_copy(0, 1, way).start()
-    for way in range(2):
-        zs_copy(1, 1, way).start()
-    each(NP, ids_copies, start)
-    each(NP, ids_copies, wait)
-    to_scalar = pltpu.make_async_copy(want_v, want_s, load_sem.at[6])
-    to_scalar.start()
-    to_scalar.wait()
-    stage(0, 0)
-    stage(1, 0)
-    arrange(0)
-    for step in range(1, 5):
-        turn(0, step)
-        stage(0, step)
-        arrange(2 * step - 1)
-        turn(1, step)
-        stage(1, step)
-        if step < 4:
-            arrange(2 * step)
-
-    load_sl.wait()
-    for p in range(2):
-        rows = sl_v[:, p * 128 : (p + 1) * 128].T
-        for half in range(2):
-            own = rows[half * BLK : (half + 1) * BLK].reshape(NX, QROWS, KDIM)
-            key_a[2 * p + half, PICKED, :, :, IDIM:] = own[:, :, :HEAD_A]
-            key_b[2 * p + half, PICKED] = own[:, :, HEAD_A:]
-    load_si.wait()
-
     def gathered(a):
         for step in range(len(spans)):
             each(NP, lambda i: [ys_copy(a, step, i)], wait)
@@ -251,9 +222,9 @@
         if step == 0:
             rows, part = h, pl.ds(0, PICKED)
         elif way == 0:
-            rows, part = x_prev, pl.ds(0, 4)
+            rows, part = x_prev, pl.ds(0, 3 + r % 2)
         else:
-            rows, part = x_next, pl.ds(4, 3)
+            rows, part = x_next, pl.ds(3 + r % 2, 4 - r % 2)
         spot = (key_b if a else key_a).at[r, part, rows]
         return remote(
             spot,
@@ -277,22 +248,61 @@
         for way in range(2):
             xs_copy(a, r, 1, way).wait_recv()
 
-    gathered(0)
-    for r in range(QBLK):
-        xs_start(0, r)
+    def z_start(a):
+        for way in range(2):
+            zs_copy(a, 1, way).start()
+
+    z_start(0)
+    each(NP, ids_copies, start)
+    each(NP, ids_copies, wait)
+    to_scalar = pltpu.make_async_copy(want_v, want_s, load_sem.at[6])
+    to_scalar.start()
+    to_scalar.wait()
+    stage(0, 0)
+    arrange(0)
+    for step in range(1, 5 + LAG):
+        if step <= 4:
+            turn(0, step)
+        if step == LAG:
+            z_start(1)
+            stage(1, 0)
+        if step <= 4:
+            stage(0, step)
+            arrange(step)
+            if step == 4:
+                gathered(0)
+                for r in range(QBLK):
+                    xs_start(0, r)
+        if step > LAG:
+            turn(1, step - LAG)
+            stage(1, step - LAG)
+            if step > 4:
+                xs_turn(0, step - 5)
+    for unit in range(5, 8):
+        arrange(unit)
+    load_sl.wait()
+    for p in range(2):
+        rows = sl_v[:, p * 128 : (p + 1) * 128].T
+        for half in range(2):
+            own = rows[half * BLK : (half + 1) * BLK].reshape(NX, QROWS, KDIM)
+            key_a[2 * p + half, PICKED, :, :, IDIM:] = own[:, :, :HEAD_A]
+            key_b[2 * p + half, PICKED] = own[:, :, HEAD_A:]
+    load_si.wait()
     gathered(1)
-    for r in range(QBLK):
+    xs_start(1, 0)
+    for r in range(LAG, QBLK):
         xs_turn(0, r)
-        xs_start(1, r)
-
-    def rs_copies(a, r):
-        src, dst = (mass_b, rs_m) if a else (logits, rs_l)
-        return remote(src.at[r], dst.at[h], rs_send.at[a, r], rs_recv.at[a, h], (seq, r))
-
-    def rs_start(a, r):
-        @pl.when(h != r)
-        def _():
-            rs_copies(a, r).start()
+        xs_start(1, r - LAG + 1)
+
+    def rs_copies(r, i):
+        peer = (h + i) % NX
+        theirs = pl.ds(pl.multiple_of(peer * QROWS, QROWS), QROWS)
+        return [
+            remote(
+                src.at[r, theirs], dst.at[r, h], rs_send.at[a, r, i], rs_recv.at[a, r, i], (seq, peer)
+            )
+            for a, (src, dst) in enumerate(((logits, rs_l), (mass_b, rs_m)))
+        ]
 
     def ikeys_of(r):
         return key_a[r, :, :, :, :IDIM].reshape(SPAN, IDIM)
@@ -319,7 +329,6 @@
             return 0
 
         lax.fori_loop(0, BLK // PART, body, 0)
-        rs_start(0, r)
 
     def make_mass(r):
         keys = jnp.concatenate(
@@ -357,52 +366,44 @@
         lax.fori_loop(0, NOCT, body, 0)
         mass = (sums[:, :BLK] + sums[:, BLK:]).T
 
-        @pl.when(h == r)
-        def _():
-            mass_o[...] = mass
-
+        mass_o[r] = mass
         mass_b[r] = mass.astype(jnp.bfloat16)
-        rs_start(1, r)
+        each(NX, lambda i: rs_copies(r, i), start)
 
     def lg_copies(r, i):
         peer = (h + i) % NX
-        return [
-            remote(lg.at[r], lg.at[r], lg_send.at[0, i], lg_recv.at[0, r], (seq, peer)),
-            remote(div.at[r], div.at[r], lg_send.at[1, i], lg_recv.at[1, r], (seq, peer)),
-        ]
+        return [remote(lg.at[r, quarter], lg.at[r, quarter], lg_send.at[r, i], lg_recv.at[r, i], (seq, peer))]
+
+    def div_copies(i):
+        peer = (h + i) % NX
+        return [remote(div.at[h], div.at[h], lg_send.at[QBLK, i], lg_recv.at[QBLK, i], (seq, peer))]
 
     def divergence_of(r):
+        each(NX, lambda i: rs_copies(r, i), wait)
+        mass_sum, logit = mass_o[r, quarter], logits[r, quarter]
         for i in range(1, NX):
-            peer = (h + i) % NX
-            for a, (src, dst) in enumerate(((logits, rs_l), (mass_b, rs_m))):
-                remote(
-                    src.at[r], dst.at[peer], rs_send.at[a, r], rs_recv.at[a, peer], (seq, peer)
-                ).wait_recv()
-        mass_sum, logit = mass_o[...], logits[r]
-        for i in range(1, NX):
-            mass_sum = mass_sum + rs_m[(h + i) % NX].astype(jnp.float32)
-            logit = logit + rs_l[(h + i) % NX]
+            mass_sum = mass_sum + rs_m[r, (h + i) % NX].astype(jnp.float32)
+            logit = logit + rs_l[r, (h + i) % NX]
         target = mass_sum * (1.0 / HEADS)
-        column = lax.broadcasted_iota(jnp.int32, (BLK, SPAN), 1)
-        token = lax.broadcasted_iota(jnp.int32, (BLK, SPAN), 0)
+        column = lax.broadcasted_iota(jnp.int32, (QROWS, SPAN), 1)
+        token = lax.broadcasted_iota(jnp.int32, (QROWS, SPAN), 0) + h * QROWS
         allowed = column - PICKED * BLK <= token
         masked = jnp.where(allowed, logit, -jnp.inf)
         shifted = masked - jnp.max(masked, axis=1, keepdims=True)
         powers = jnp.exp(shifted)
         total = jnp.sum(powers, axis=1, keepdims=True)
         model = powers / total
+        lg[r, quarter] = jnp.where(allowed, model - target, 0.0).astype(jnp.bfloat16)
+        each(NX, lambda i: lg_copies(r, i), start)
         log_model = jnp.where(allowed, shifted - jnp.log(total), 0.0)
         safe = jnp.where(target > 0, target, 1.0)
         pointwise = jnp.where(allowed, target * (jnp.log(safe) - log_model), 0.0)
         divergence = jnp.sum(pointwise, axis=1, keepdims=True)
-        lg[r] = jnp.where(allowed, model - target, 0.0).astype(jnp.bfloat16)
-        each(NX, lambda i: lg_copies(r, i)[:1], start)
-        diagonal = lax.broadcasted_iota(jnp.int32, (BLK, 128), 0) == lax.broadcasted_iota(
-            jnp.int32, (BLK, 128), 1
-        )
-        in_lanes = jnp.sum(jnp.where(diagonal, divergence, 0.0), axis=0, keepdims=True)
-        div[r] = jnp.broadcast_to(in_lanes, (8, 128))
-        each(NX, lambda i: lg_copies(r, i)[1:], start)
+        spot = lax.broadcasted_iota(jnp.int32, (QROWS, 128), 1) == h * QROWS + (
+            lax.broadcasted_iota(jnp.int32, (QROWS, 128), 0)
+        )
+        in_lanes = jnp.sum(jnp.where(spot, divergence, 0.0), axis=0, keepdims=True)
+        return jnp.where(lax.broadcasted_iota(jnp.int32, (8, 128), 0) == r, in_lanes, 0.0)
 
     def k_copy(i, r):
         peer = (h + i) % NX
@@ -414,11 +415,15 @@
         rows = pl.ds(r * BLK, BLK)
         return pltpu.make_async_copy(qgrad_v.at[rows], out_qgrad.at[rows], out_sem.at[r])
 
+    stores = [
+        pltpu.make_async_copy(src, dst, out_sem.at[QBLK + n])
+        for n, (src, dst) in enumerate(
+            ((ggrad_v, out_ggrad), (div_v, out_div), (own_g, out_own), (cache_g, out_cache))
+        )
+    ]
+
     def backward(r):
-        @pl.when(h != r)
-        def _():
-            lg_copies(r, 1)[0].wait_recv()
-
+        each(NX, lambda i: lg_copies(r, i), wait)
         ikeys = ikeys_of(r)
         kgrad[...] = jnp.zeros_like(kgrad)
         ggrad_t[...] = jnp.zeros_like(ggrad_t)
@@ -459,12 +464,7 @@
             kquarter[r, j] = kgrad[pl.ds(pl.multiple_of(j * BLK + h * QROWS, QROWS), QROWS)]
         each(NX, lambda i: [k_copy(i, r)], start)
         qgrad_copy(r).start()
-        out_ggrad[:, r * BLK : (r + 1) * BLK] = ggrad_t[:, :BLK]
-
-    def owner_step(r):
-        @pl.when(h == r)
-        def _():
-            divergence_of(r)
+        ggrad_v[:, r * BLK : (r + 1) * BLK] = ggrad_t[:, :BLK]
 
     load_qi.wait()
     load_gains.wait()
@@ -473,16 +473,21 @@
         make_logits(r)
         if r < QBLK - 1:
             xs_turn(1, r)
+            if r + QBLK - LAG + 1 < QBLK:
+                xs_start(1, r + QBLK - LAG + 1)
+    tiles = []
     for r in range(QBLK):
         xs_done(1, r)
         make_mass(r)
         if r == 0:
             xs_turn(1, QBLK - 1)
         if r >= 1:
-            owner_step(r - 1)
+            tiles.append(divergence_of(r - 1))
         if r >= 2:
             backward(r - 2)
-    owner_step(QBLK - 1)
+    tiles.append(divergence_of(QBLK - 1))
+    div[h] = sum(tiles[1:], tiles[0])
+    each(NX, div_copies, start)
     backward(QBLK - 2)
     backward(QBLK - 1)
 
@@ -494,6 +499,8 @@
         own_g[r, h] = total[PICKED]
         slots[pl.ds(r * 8, 8)] = total.astype(jnp.bfloat16)
 
+    stores[0].start()
+
     def put_back(p, _):
         for place in range(NZ):
             slot = jnp.maximum(want_s[me, 1, p * NZ + place], 0)
@@ -502,13 +509,23 @@
 
     lax.fori_loop(0, NP, put_back, 0)
 
-    def y_copies(i):
+    groups = ((5, 3), (3, 2), (0, 3))
+
+    def y_copies(g, i):
         peer = (me + i) % NP
+        places = pl.ds(groups[g][0], groups[g][1])
         return [
-            remote(ret_s.at[peer], ret_r.at[me], y_send.at[i], y_recv.at[i], (z * NP + peer, h))
+            remote(
+                ret_s.at[peer, places],
+                ret_r.at[me, places],
+                y_send.at[g, i],
+                y_recv.at[g, i],
+                (z * NP + peer, h),
+            )
         ]
 
-    each(NP, y_copies, start)
+    for g in range(3):
+        each(NP, lambda i: y_copies(g, i), start)
 
     def own_copies(i):
         peer = (h + i) % NX
@@ -516,7 +533,6 @@
 
     each(NX, own_copies, start)
     ret_r[me] = ret_s[me]
-    each(NP, y_copies, wait)
 
     def z_copies(place):
         peer = ((z + place_offset(place)) % NZ) * NP + me
@@ -539,7 +555,9 @@
 
         return 0
 
-    lax.fori_loop(0, NZ, add_up, 0)
+    for g, (first, count) in enumerate(groups):
+        each(NP, lambda i: y_copies(g, i), wait)
+        lax.fori_loop(0, count, lambda i, _: add_up(first + count - 1 - i, 0), 0)
 
     for step in range(1, 5):
         for way in range(2):
@@ -550,22 +568,15 @@
             for step in range(2):
                 for way in range(2):
                     xs_copy(a, r, step, way).wait_send()
-    for r in range(QBLK):
-
-        @pl.when(h != r)
-        def _():
-            rs_copies(0, r).wait_send()
-            rs_copies(1, r).wait_send()
-            lg_copies(r, 1)[1].wait_recv()
-
-        @pl.when(h == r)
-        def _():
-            each(NX, lambda i: lg_copies(r, i), wait_send)
-
-    out_div[...] = div[...]
-    for r in range(QBLK):
-        qgrad_copy(r).wait()
-
+    each(NX, div_copies, wait)
+    spread = div[0] + div[1] + div[2] + div[3]
+    for p in range(2):
+        div_v[p : p + 1] = jnp.concatenate(
+            [spread[2 * p : 2 * p + 1, :BLK], spread[2 * p + 1 : 2 * p + 2, :BLK]], axis=1
+        )
+    stores[1].start()
+    each(NX, own_copies, wait)
+    stores[2].start()
     each(NZ, z_copies, wait)
     cache_sum = z_part[0].astype(jnp.float32)
     for place in range(1, NZ):
@@ -579,14 +590,26 @@
         ]
 
     each(NX, cache_copies, start)
-    each(NX, own_copies, wait)
-    own_store = pltpu.make_async_copy(own_g, out_own, out_sem.at[4])
-    own_store.start()
     each(NX, cache_copies, wait)
-    cache_store = pltpu.make_async_copy(cache_g, out_cache, out_sem.at[5])
-    cache_store.start()
-    own_store.wait()
-    cache_store.wait()
+    stores[3].start()
+    for r in range(QBLK):
+        qgrad_copy(r).wait()
+    for store in stores:
+        store.wait()
+
+
+def emit_kernel(*refs):
+    ins, outs, held, sems = refs[:5], refs[5:10], refs[10:15], refs[15]
+    order = (1, 3, 4, 2, 0)
+    loads = [pltpu.make_async_copy(ins[n], held[n], sems.at[0, n]) for n in range(5)]
+    stores = [pltpu.make_async_copy(held[n], outs[n], sems.at[1, n]) for n in range(5)]
+    for n in order:
+        loads[n].start()
+    for n in order:
+        loads[n].wait()
+        stores[n].start()
+    for n in order:
+        stores[n].wait()
 
 
 def per_device(
@@ -600,19 +623,19 @@
     block_ids,
 ):
     f32, bf16, sem, V = jnp.float32, jnp.bfloat16, pltpu.SemaphoreType.DMA, pltpu.VMEM
-    vmem = pl.BlockSpec(memory_space=pltpu.VMEM)
-    any_space = pl.BlockSpec(memory_space=pl.ANY)
-    divergence, qgrad, ggrad, cache_grad, own_grad = pl.pallas_call(
+    any_space = pl.BlockSpec(memory_space=pltpu.HBM)
+    shapes = (
+        jax.ShapeDtypeStruct((2, 128), f32),
+        jax.ShapeDtypeStruct((ROWS, IHEADS, IDIM), bf16),
+        jax.ShapeDtypeStruct((IHEADS, ROWS), f32),
+        jax.ShapeDtypeStruct((8, NX, QROWS, IDIM), f32),
+        jax.ShapeDtypeStruct((QBLK, NX, QROWS, IDIM), f32),
+    )
+    results = pl.pallas_call(
         kernel,
-        out_shape=(
-            jax.ShapeDtypeStruct((QBLK, 8, 128), f32),
-            jax.ShapeDtypeStruct((ROWS, IHEADS, IDIM), bf16),
-            jax.ShapeDtypeStruct((IHEADS, ROWS), f32),
-            jax.ShapeDtypeStruct((8, NX, QROWS, IDIM), f32),
-            jax.ShapeDtypeStruct((QBLK, NX, QROWS, IDIM), f32),
-        ),
+        out_shape=shapes,
         in_specs=[pl.BlockSpec(memory_space=pltpu.SMEM)] + [any_space] * 7,
-        out_specs=(vmem, any_space, vmem, any_space, any_space),
+        out_specs=(any_space,) * 5,
         scratch_shapes=[
             *[V((8, QROWS, WIDE_A), bf16)] * NZ,
             *[V((8, QROWS, WIDE_B), bf16)] * NZ,
@@ -631,11 +654,11 @@
             V((ROWS, IHEADS, IDIM), bf16),
             V((IHEADS, ROWS), f32),
             V((SPAN, 128), f32),
-            V((BLK, SPAN), f32),
+            V((QBLK, BLK, SPAN), f32),
             V((QBLK, BLK, SPAN), bf16),
             V((QBLK, BLK, SPAN), f32),
-            V((NX, BLK, SPAN), bf16),
-            V((NX, BLK, SPAN), f32),
+            V((QBLK, NX, QROWS, SPAN), bf16),
+            V((QBLK, NX, QROWS, SPAN), f32),
             V((QBLK, BLK, SPAN), bf16),
             V((QBLK, 8, 128), f32),
             V((SPAN, IDIM), f32),
@@ -649,11 +672,13 @@
             V((NZ, 8, QROWS, IDIM), bf16),
             V((8, NX, QROWS, IDIM), f32),
             V((QBLK, NX, QROWS, IDIM), f32),
+            V((IHEADS, 128), f32),
             V((ROWS, IHEADS, IDIM), bf16),
-            V((IHEADS, 128), f32),
+            V((IHEADS, ROWS), f32),
+            V((2, 128), f32),
             sem((7,)),
             sem((NOCT,)),
-            sem((6,)),
+            sem((8,)),
             sem((NP,)),
             sem((NP,)),
             sem((2, 2, 5)),
@@ -662,21 +687,21 @@
             sem((2, 5, NP)),
             sem((2, QBLK, 2, 2)),
             sem((2, QBLK, 2, 2)),
-            sem((2, QBLK)),
-            sem((2, NX)),
-            sem((2, NX)),
-            sem((2, QBLK)),
+            sem((2, QBLK, NX)),
+            sem((2, QBLK, NX)),
+            sem((QBLK + 1, NX)),
+            sem((QBLK + 1, NX)),
             sem((NX, QBLK)),
             sem((NX, QBLK)),
-            sem((NP,)),
-            sem((NP,)),
+            sem((3, NP)),
+            sem((3, NP)),
             sem((NZ,)),
             sem((NZ,)),
             sem((2, NX)),
             sem((2, NX)),
         ],
         compiler_params=pltpu.CompilerParams(
-            collective_id=0, has_side_effects=True, vmem_limit_bytes=60 << 20
+            collective_id=0, has_side_effects=True, vmem_limit_bytes=58 << 20
         ),
         name="indexer_kl",
     )(
@@ -689,8 +714,17 @@
         query_index,
         index_gains.T,
     )
+    divergence, qgrad, ggrad, cache_grad, own_grad = pl.pallas_call(
+        emit_kernel,
+        out_shape=shapes,
+        in_specs=[any_space] * 5,
+        out_specs=(any_space,) * 5,
+        scratch_shapes=[*[V(a.shape, a.dtype) for a in shapes], sem((2, 5))],
+        compiler_params=pltpu.CompilerParams(vmem_limit_bytes=58 << 20),
+        name="emit",
+    )(*results)
     return (
-        divergence[:, 0, :BLK].reshape(ROWS),
+        divergence.reshape(ROWS),
         qgrad,
         ggrad.T,
         cache_grad.reshape(CACHED, IDIM),

time: 130 us -> 116 us (0.89)
  local copies, waits for them, and re-layouts: 8.31 us -> 0 us
  Pallas kernels: 121 us -> 114 us
    unnamed x4 -> x0, local copies, waits for them, and re-layouts: 6.93 us -> none
    pallas_call x1 -> x2, Pallas kernels: 121 us -> 114 us  [the longest x1 111 us: per_device(): pl.pallas_call(kernel, out_shape=shapes, in_specs=[pl.BlockSpec(memory_sp...]
where the time goes in v3:
time: 116 us; the launch traced here: 115 us
  Pallas kernels  114 us (98%)
    pallas_call x1, Pallas kernels, per_device(): pl.pallas_call(kernel, out_shape=shapes, in_specs=[pl.BlockSpec(memory_sp...  111 us
    pallas_call x1, Pallas kernels, per_device(): pl.pallas_call(emit_kernel, out_shape=shapes, in_specs=[any_space] * 5, o...  2.4 us

profile of v3, /device:TPU:32, one launch (start us, length us, event | category | flops | bytes accessed | tf_op | source)
XLA Modules:
  0.0 114.5 jit_solution(8921247527606996303)
XLA Ops:
  0.6 111.5 %indexer_kl.1 = (f32[2,128]{1,0:T(2,128)}, bf16[256,16,128]{2,1,0:T(8,128)(2,1)}, f32[16,256]{1,0:T(8,128)}, f32[8,4,16,128]{3,2,1,0:T(8,128)}, f32[4,4,16,128]{3,2,1,0:T(8,128)}) custom-call(s32[4,7]{1,0:T(4,128)} %ids.1, bf16[576,512]{1,0:T(8,128)(2,1)} %bitcast.11, bf16[8,4,16,128]{3,2,1,0:T(8,128)(2,1)} %bitcast.13, bf16[576,256]{1,0:T(8,128)(2,1)} %bitcast.12, ...), custom_call_target="tpu_custom_call" | custom-call | tf_op jit(solution)/shard_map/indexer_kl/pallas_call | solution.py:634
  112.1 2.4 %emit.1 = (f32[2,128]{1,0:T(2,128)}, bf16[256,16,128]{2,1,0:T(8,128)(2,1)}, f32[16,256]{1,0:T(8,128)}, f32[8,4,16,128]{3,2,1,0:T(8,128)}, f32[4,4,16,128]{3,2,1,0:T(8,128)}) custom-call(f32[2,128]{1,0:T(2,128)} %get-tuple-element.15.refs_0_, bf16[256,16,128]{2,1,0:T(8,128)(2,1)} %get-tuple-element.16.refs_1_, f32[16,256]{1,0:T(8,128)} %get-tuple-element.17.refs_2_, ...), custom_call_target="tpu_custom_call" | custom-call | tf_op jit(solution)/shard_map/emit/pallas_call | solution.py:717

commit v4 on v3

--- a/solution.py
+++ b/solution.py
@@ -254,12 +254,19 @@
 
     z_start(0)
     each(NP, ids_copies, start)
+    load_sl.wait()
+    for p in range(2):
+        rows = sl_v[:, p * 128 : (p + 1) * 128].T
+        for half in range(2):
+            own = rows[half * BLK : (half + 1) * BLK].reshape(NX, QROWS, KDIM)
+            key_a[2 * p + half, PICKED, :, :, IDIM:] = own[:, :, :HEAD_A]
+            key_b[2 * p + half, PICKED] = own[:, :, HEAD_A:]
+    arrange(0)
     each(NP, ids_copies, wait)
     to_scalar = pltpu.make_async_copy(want_v, want_s, load_sem.at[6])
     to_scalar.start()
     to_scalar.wait()
     stage(0, 0)
-    arrange(0)
     for step in range(1, 5 + LAG):
         if step <= 4:
             turn(0, step)
@@ -268,7 +275,6 @@
             stage(1, 0)
         if step <= 4:
             stage(0, step)
-            arrange(step)
             if step == 4:
                 gathered(0)
                 for r in range(QBLK):
@@ -278,15 +284,8 @@
             stage(1, step - LAG)
             if step > 4:
                 xs_turn(0, step - 5)
-    for unit in range(5, 8):
-        arrange(unit)
-    load_sl.wait()
-    for p in range(2):
-        rows = sl_v[:, p * 128 : (p + 1) * 128].T
-        for half in range(2):
-            own = rows[half * BLK : (half + 1) * BLK].reshape(NX, QROWS, KDIM)
-            key_a[2 * p + half, PICKED, :, :, IDIM:] = own[:, :, :HEAD_A]
-            key_b[2 * p + half, PICKED] = own[:, :, HEAD_A:]
+        if step <= 4:
+            arrange(step)
     load_si.wait()
     gathered(1)
     xs_start(1, 0)
@@ -363,7 +362,7 @@
                 sums[lo:hi] += fold
             return 0
 
-        lax.fori_loop(0, NOCT, body, 0)
+        lax.fori_loop(0, NOCT, body, 0, unroll=NOCT)
         mass = (sums[:, :BLK] + sums[:, BLK:]).T
 
         mass_o[r] = mass
@@ -472,6 +471,7 @@
         xs_done(0, r)
         make_logits(r)
         if r < QBLK - 1:
+            arrange(5 + r)
             xs_turn(1, r)
             if r + QBLK - LAG + 1 < QBLK:
                 xs_start(1, r + QBLK - LAG + 1)

time: 116 us -> 113 us (0.974)
  Pallas kernels: 114 us -> 111 us
    pallas_call x1, Pallas kernels: 111 us -> 109 us  [per_device(): pl.pallas_call(kernel, out_shape=shapes, in_specs=[pl.BlockSpec(memory_sp...]
where the time goes in v4:
time: 113 us; the launch traced here: 112 us
  Pallas kernels  111 us (98%)
    pallas_call x1, Pallas kernels, per_device(): pl.pallas_call(kernel, out_shape=shapes, in_specs=[pl.BlockSpec(memory_sp...  109 us
    pallas_call x1, Pallas kernels, per_device(): pl.pallas_call(emit_kernel, out_shape=shapes, in_specs=[any_space] * 5, o...  2.4 us

profile of v4, /device:TPU:32, one launch (start us, length us, event | category | flops | bytes accessed | tf_op | source)
XLA Modules:
  0.0 112.0 jit_solution(17407626088918199316)
XLA Ops:
  0.6 108.8 %indexer_kl.1 = (f32[2,128]{1,0:T(2,128)}, bf16[256,16,128]{2,1,0:T(8,128)(2,1)}, f32[16,256]{1,0:T(8,128)}, f32[8,4,16,128]{3,2,1,0:T(8,128)}, f32[4,4,16,128]{3,2,1,0:T(8,128)}) custom-call(s32[4,7]{1,0:T(4,128)} %ids.1, bf16[576,512]{1,0:T(8,128)(2,1)} %bitcast.11, bf16[8,4,16,128]{3,2,1,0:T(8,128)(2,1)} %bitcast.13, bf16[576,256]{1,0:T(8,128)(2,1)} %bitcast.12, ...), custom_call_target="tpu_custom_call" | custom-call | tf_op jit(solution)/shard_map/indexer_kl/pallas_call | solution.py:634
  109.4 2.4 %emit.1 = (f32[2,128]{1,0:T(2,128)}, bf16[256,16,128]{2,1,0:T(8,128)(2,1)}, f32[16,256]{1,0:T(8,128)}, f32[8,4,16,128]{3,2,1,0:T(8,128)}, f32[4,4,16,128]{3,2,1,0:T(8,128)}) custom-call(f32[2,128]{1,0:T(2,128)} %get-tuple-element.15.refs_0_, bf16[256,16,128]{2,1,0:T(8,128)(2,1)} %get-tuple-element.16.refs_1_, f32[16,256]{1,0:T(8,128)} %get-tuple-element.17.refs_2_, ...), custom_call_target="tpu_custom_call" | custom-call | tf_op jit(solution)/shard_map/emit/pallas_call | solution.py:717
